TPU v7x, 256 devices: a whole 4x4x8 slice. The times are simulated.
256 devices in a mesh: dap: 16 (over x_hi, z), dp: 16 (over y, x_lo, core).
Axes of the slice: x: 4 (x_hi: 2, x_lo: 2; x = x_hi * 2 + x_lo), y: 4, z: 8, core: 2. Of those that a mesh axis runs over, the one named last changes fastest.
Arguments:
- alignment: bfloat16 [2048, 256, 256], P(('dp', 'dap')), parts along dimension 0, may hold values from -6 to 6
- pair_state: bfloat16 [4096, 256, 128], P(('dp', 'dap')), parts along dimension 0, may hold values from -6 to 6
- residue_present_mask: int32 [4096], P('dp'), parts along dimension 0, may hold values 0 or 1
- alignment_row_mask: int32 [2048], P('dp'), parts along dimension 0, may hold values 0 or 1
- row_query_weight: bfloat16 [256, 256], replicated
- row_key_weight: bfloat16 [256, 256], replicated
- row_value_weight: bfloat16 [256, 256], replicated, may hold values from -0.375 to 0.375
- row_gate_weight: bfloat16 [256, 256], replicated, may hold values from -0.375 to 0.375
- row_output_weight: bfloat16 [256, 256], replicated, may hold values from -1 to 1
- pair_bias_weight: bfloat16 [128, 8], replicated, may hold values from -1.1953125 to 1.1953125
- column_query_weight: bfloat16 [256, 256], replicated
- column_key_weight: bfloat16 [256, 256], replicated
- column_value_weight: bfloat16 [256, 256], replicated, may hold values from -0.375 to 0.375
- column_gate_weight: bfloat16 [256, 256], replicated, may hold values from -0.375 to 0.375
- column_output_weight: bfloat16 [256, 256], replicated, may hold values from -1 to 1
- triangle_left_weight: bfloat16 [128, 128], replicated, may hold values from -0.5 to 0.5
- triangle_right_weight: bfloat16 [128, 128], replicated, may hold values from -0.5 to 0.5
- triangle_gate_weight: bfloat16 [128, 128], replicated, may hold values from -0.5 to 0.5
- triangle_output_weight: bfloat16 [128, 128], replicated, may hold values from -0.5 to 0.5
- transition_input_weight: bfloat16 [128, 512], replicated, may hold values from -0.5 to 0.5
- transition_output_weight: bfloat16 [512, 128], replicated, may hold values from -0.25 to 0.25
Outputs:
- alignment_updated: bfloat16 [2048, 256, 256], P('dp', 'dap'), parts along dimension 0
- pair_next: bfloat16 [4096, 256, 128], P(('dp', 'dap')), parts along dimension 0
There are 16 independent parts, one for each index of `dp`. A program takes and returns all parts, laid end to end along the dimension named above; an argument that names none is the same for every part. Nothing has to cross between parts.
All inputs are finite; a program needn't handle non-finite values.
Results may differ from a plain program's by a relative error of at most 0.012.
The roundings to bfloat16 on the way count: a program that leaves them out, or rounds other values in their place, can miss the bound.
Values may be sent and summed in bfloat16 or wider, within the bound.
A program may use at most 128 MiB of HBM per device.

v0:
```python
import jax
import jax.numpy as jnp
from jax import lax
from jax.sharding import PartitionSpec as P

DH = 32


epsilon = 1e-05
masked_score = -1000000000.0


def layer_normalize(values):
    values = values.astype(jnp.float32)
    center = values - jnp.mean(values, axis=-1, keepdims=True)
    variance = jnp.mean(center * center, axis=-1, keepdims=True)
    return (center * lax.rsqrt(variance + epsilon)).astype(jnp.bfloat16)


def project(values, weight):
    flattened = values.reshape(-1, values.shape[-1])
    result = jnp.dot(flattened, weight, preferred_element_type=jnp.float32)
    return result.reshape(values.shape[:-1] + (weight.shape[1],))


def gated_head_attention(
    normalized_input, bias_term, key_bias, w_query, w_key, w_value, w_gate, w_out
):
    batch_rows, length = (normalized_input.shape[0], normalized_input.shape[1])
    head_count = w_query.shape[1] // DH
    query_rows = (
        (project(normalized_input, w_query) * DH ** (-0.5))
        .astype(jnp.bfloat16)
        .reshape(batch_rows, length, head_count, DH)
    )
    key_rows = (
        project(normalized_input, w_key)
        .astype(jnp.bfloat16)
        .reshape(batch_rows, length, head_count, DH)
    )
    value_rows = (
        project(normalized_input, w_value)
        .astype(jnp.bfloat16)
        .reshape(batch_rows, length, head_count, DH)
    )
    gate_rows = jax.nn.sigmoid(project(normalized_input, w_gate))
    scores = jnp.einsum("bihd,bjhd->bhij", query_rows, key_rows, preferred_element_type=jnp.float32)
    scores = scores + bias_term + key_bias[None, None, None, :]
    row_max = jnp.max(scores, axis=-1, keepdims=True)
    expo = jnp.exp(scores - row_max)
    row_total = jnp.sum(expo, axis=-1, keepdims=True)
    probabilities = (expo / row_total).astype(jnp.bfloat16)
    mixture = jnp.einsum(
        "bhij,bjhd->bihd", probabilities, value_rows, preferred_element_type=jnp.float32
    )
    gated_rows = (mixture.reshape(batch_rows, length, head_count * DH) * gate_rows).astype(
        jnp.bfloat16
    )
    return project(gated_rows, w_out)


def shards(
    alignment,
    pair_state,
    residue_present_mask,
    alignment_row_mask,
    row_query_weight,
    row_key_weight,
    row_value_weight,
    row_gate_weight,
    row_output_weight,
    pair_bias_weight,
    column_query_weight,
    column_key_weight,
    column_value_weight,
    column_gate_weight,
    column_output_weight,
    triangle_left_weight,
    triangle_right_weight,
    triangle_gate_weight,
    triangle_output_weight,
    transition_input_weight,
    transition_output_weight,
):
    own_rows = pair_state.shape[0]
    device_index = lax.axis_index("dap")
    residue_live = residue_present_mask.astype(jnp.float32)
    sequence_present = alignment_row_mask.astype(jnp.float32)
    residue_mask_bias = (1.0 - residue_live) * masked_score
    seq_bias = (1.0 - sequence_present) * masked_score
    own_live = lax.dynamic_slice_in_dim(residue_live, device_index * own_rows, own_rows)
    pair_norm = layer_normalize(pair_state)
    own_left = (
        project(pair_norm, triangle_left_weight)
        * (own_live[:, None] * residue_live[None, :])[:, :, None]
    ).astype(jnp.bfloat16)
    left_sides = jnp.transpose(own_left, (2, 0, 1))
    pair_bias = lax.all_gather(
        jnp.transpose(project(pair_norm, pair_bias_weight), (2, 0, 1)).astype(jnp.bfloat16),
        "dap",
        axis=1,
        tiled=True,
    )
    right = (
        project(pair_norm, triangle_right_weight)
        * (own_live[:, None] * residue_live[None, :])[:, :, None]
    ).astype(jnp.bfloat16)
    combined = jnp.einsum(
        "cik,cjk->cij",
        left_sides,
        lax.all_gather(jnp.transpose(right, (2, 0, 1)), "dap", axis=1, tiled=True),
        preferred_element_type=jnp.float32,
    )
    combined_norm = layer_normalize(jnp.transpose(combined, (1, 2, 0)))
    gate_values = jax.nn.sigmoid(project(pair_norm, triangle_gate_weight))
    pair_mid = (
        pair_state.astype(jnp.float32)
        + project(combined_norm, triangle_output_weight) * gate_values
    ).astype(jnp.bfloat16)
    trans_norm = layer_normalize(pair_mid)
    hidden = jax.nn.relu(project(trans_norm, transition_input_weight)).astype(jnp.bfloat16)
    pair_next = (pair_mid.astype(jnp.float32) + project(hidden, transition_output_weight)).astype(
        jnp.bfloat16
    )
    bias_expanded = pair_bias.astype(jnp.float32)[None]
    alignment_normalized = layer_normalize(alignment)
    row_attention_update = gated_head_attention(
        alignment_normalized,
        bias_expanded,
        residue_mask_bias,
        row_query_weight,
        row_key_weight,
        row_value_weight,
        row_gate_weight,
        row_output_weight,
    )
    alignment_middle = (alignment.astype(jnp.float32) + row_attention_update).astype(jnp.bfloat16)
    transposed_alignment = lax.all_to_all(
        alignment_middle, "dap", split_axis=1, concat_axis=0, tiled=True
    )
    column_normalize = layer_normalize(jnp.transpose(transposed_alignment, (1, 0, 2)))
    column_attention_update = gated_head_attention(
        column_normalize,
        0.0,
        seq_bias,
        column_query_weight,
        column_key_weight,
        column_value_weight,
        column_gate_weight,
        column_output_weight,
    )
    alignment_updated = (
        transposed_alignment.astype(jnp.float32) + jnp.transpose(column_attention_update, (1, 0, 2))
    ).astype(jnp.bfloat16)
    return (alignment_updated, pair_next)


def solution(mesh):
    in_specs = (
        P(("dp", "dap"), None, None),
        P(("dp", "dap"), None, None),
        P("dp"),
        P("dp"),
        P(),
        P(),
        P(),
        P(),
        P(),
        P(),
        P(),
        P(),
        P(),
        P(),
        P(),
        P(),
        P(),
        P(),
        P(),
        P(),
        P(),
    )
    out_specs = (P("dp", "dap", None), P(("dp", "dap"), None, None))
    return jax.shard_map(shards, mesh=mesh, in_specs=in_specs, out_specs=out_specs, check_vma=False)
```

profile of v0, /device:TPU:6, one launch (start us, length us, event | category | flops | bytes accessed | tf_op | source)
XLA Modules:
  0.0 366.6 jit_solution(4810724858560516697)
XLA Ops:
  7.2 0.0 copy-start
  7.2 0.0 all-gather.3.cloned.1.call-start
  7.3 1.5 copy.95
  8.8 0.0 copy-start.15
  8.8 0.2 convert_reduce_fusion.1
  9.0 0.3 fusion.25
  9.3 0.1 dynamic_slice.3
  9.4 0.1 add_rsqrt_fusion.2
  9.5 1.0 fusion.35
  10.4 0.0 all-gather.3.cloned.1.call-update
  10.5 0.0 all-gather.5.cloned.1.call-start
  10.5 1.0 fusion.34
  11.6 0.0 copy-start.2
  11.6 1.3 copy.109
  12.9 0.0 all-gather.5.cloned.1.call-update
  12.9 0.3 convert_reduce_fusion.2
  13.3 0.0 copy-start.5
  13.3 0.6 fusion.27
  14.0 0.0 copy-start.6
  14.0 2.1 multiply_convert_fusion.7
  16.1 2.1 convolution_convert_fusion.2
  18.2 2.1 convolution_convert_fusion.3
  20.2 70.6 %all-gather.3.cloned.1.call-done = bf16[8,256,256]{2,0,1:T(8,128)(2,1)} async-done(((bf16[8,16,256]{2,0,1:T(8,128)(2,1)}), bf16[8,256,256]{2,0,1:T(8,128)(2,1)}) %all-gather.3.cloned.1.call-update) | async-done | bytes 1048592 | tf_op jit(solution)/shard_map/all_gather | solution.py:98
  90.8 2.8 copy.97
  93.6 10.9 %fusion.82 = (f32[8,8,256]{2,1,0:T(8,128)S(1)}, f32[8,8,256,256]{2,3,1,0:T(8,128)}) fusion(f32[256]{0:T(256)S(1)} %subtract_multiply_fusion, f32[8,256,256]{1,2,0:T(8,128)} %copy.97, bf16[8,256,8,32]{1,3,2,0:T(8,128)(2,1)} %bitcast.131, bf16[8,256,8,32]{1,3,2,0:T(8,128)(2,1)} %bitcast.132), kind=kOutput, calls=%fused_computation.111 | convolution fusion | flops 285212928 | bytes 21038080 | tf_op jit(solution)/shard_map/sub | solution.py:50
  104.6 9.4 %fusion.7 = f32[8,8,32,256]{3,2,1,0:T(8,128)} fusion(bf16[8,256,8,32]{1,3,2,0:T(8,128)(2,1)} %bitcast.130, f32[8,8,256,256]{2,3,1,0:T(8,128)} %get-tuple-element.11, f32[8,8,256]{2,1,0:T(8,128)S(1)} %get-tuple-element.10), kind=kOutput, calls=%fused_computation.13 | convolution fusion | flops 276824064 | bytes 19988480 | tf_op jit(solution)/shard_map/bhij,bjhd->bihd/dot_general | solution.py:53
  114.0 3.0 copy.99
  117.0 2.6 fusion.29
  119.6 0.0 copy-start.16
  119.6 1.6 copy.100
  121.2 7.7 %all-to-all-start = ((bf16[8,256,256]{2,0,1:T(8,128)(2,1)}), bf16[8,256,256]{2,0,1:T(8,128)(2,1)S(1)}, u32[]{:S(2)}, u32[]{:S(2)}) async-start(bf16[8,256,256]{2,0,1:T(8,128)(2,1)} %copy.100), calls=%async_computation | async-start | bytes 2097152 | tf_op jit(solution)/shard_map/all_to_all | solution.py:138
  128.9 0.0 copy-start.19
  128.9 1.0 fusion.33
  129.9 1.7 copy.110
  131.7 33.6 %all-to-all-done = bf16[8,256,256]{2,0,1:T(8,128)(2,1)S(1)} async-done(((bf16[8,256,256]{2,0,1:T(8,128)(2,1)}), bf16[8,256,256]{2,0,1:T(8,128)(2,1)S(1)}, u32[]{:S(2)}, u32[]{:S(2)}) %all-to-all-start) | async-done | bytes 1048608 | tf_op jit(solution)/shard_map/all_to_all | solution.py:138
  165.3 0.2 bitcast_convert_fusion
  165.5 0.0 copy-start.9
  165.5 0.3 bitcast_reduce_fusion.1
  165.9 0.6 multiply_reduce_fusion.1
  166.5 1.8 convolution_convert_fusion
  168.3 1.6 copy.104
  169.9 1.8 multiply_convert_fusion.4
  171.7 2.4 copy.103
  174.1 1.7 convolution_convert_fusion.1
  175.8 2.3 copy.102
  178.1 8.0 %fusion.83 = (f32[16,8,128]{2,1,0:T(8,128)S(1)}, f32[16,8,128,128]{2,3,1,0:T(8,128)}) fusion(f32[128]{0:T(128)S(1)} %subtract_multiply_fusion.1, bf16[16,128,8,32]{1,3,2,0:T(8,128)(2,1)} %bitcast.128, bf16[16,128,8,32]{1,3,2,0:T(8,128)(2,1)S(1)} %bitcast.127), kind=kOutput, calls=%fused_computation.112 | convolution fusion | flops 140509312 | bytes 10551808 | tf_op jit(solution)/shard_map/sub | solution.py:50
  186.2 7.1 %fusion.14 = f32[16,8,32,128]{3,2,1,0:T(8,128)} fusion(bf16[16,128,8,32]{1,3,2,0:T(8,128)(2,1)} %bitcast.129, f32[16,8,128,128]{2,3,1,0:T(8,128)} %get-tuple-element.13, f32[16,8,128]{2,1,0:T(8,128)S(1)} %get-tuple-element.12), kind=kOutput, calls=%fused_computation.19 | convolution fusion | flops 138412032 | bytes 11599872 | tf_op jit(solution)/shard_map/bhij,bjhd->bihd/dot_general | solution.py:53
  193.3 3.0 copy.106
  196.3 2.7 fusion.32
  199.0 1.6 copy.118
  200.5 137.0 %all-gather.5.cloned.1.call-done = bf16[128,256,256]{2,0,1:T(8,128)(2,1)} async-done(((bf16[128,16,256]{2,0,1:T(8,128)(2,1)}), bf16[128,256,256]{2,0,1:T(8,128)(2,1)}) %all-gather.5.cloned.1.call-update) | async-done | bytes 16777232 | tf_op jit(solution)/shard_map/all_gather | solution.py:111
  337.5 15.0 %bitcast_reduce_fusion = (f32[16,256]{1,0:T(8,128)S(1)}, f32[128,16,256]{2,1,0:T(8,128)S(1)}) fusion(bf16[128,16,256]{2,1,0:T(8,128)(2,1)} %copy.110, bf16[128,256,256]{2,0,1:T(8,128)(2,1)} %all-gather.5.cloned.1.call-done), kind=kOutput, calls=%fused_computation.46 | convolution fusion | flops 268955648 | bytes 19939328 | tf_op jit(solution)/shard_map/cik,cjk->cij/dot_general | solution.py:108
  352.5 0.3 multiply_reduce_fusion
  352.8 0.3 multiply_convert_fusion
  353.1 0.4 copy-done.3
  353.6 0.5 fusion.38
  354.1 0.3 copy-done.17
  354.3 0.0 copy-start.13
  354.4 0.0 copy-start.14
  354.4 1.1 convert_reduce_fusion
  355.5 0.3 fusion.23
  355.8 0.0 copy-start.1
  355.8 2.6 fusion.31
  358.4 1.3 copy.119
  (39 shorter events, 0.1 us)
Async XLA Ops:
  7.2 6.8 %copy-start = (bf16[256,256]{1,0:T(8,128)(2,1)S(1)}, bf16[256,256]{1,0:T(8,128)(2,1)}, u32[]{:S(2)}) copy-start(bf16[256,256]{1,0:T(8,128)(2,1)} %param.25) | copy-start | bytes 393220
  7.2 83.6 %all-gather.3.cloned.1.call-start = ((), (), s32[]{:S(2)}) async-start(), calls=%async_computation.1 | async-start | bytes 1114112 | tf_op jit(solution)/shard_map/all_gather | solution.py:98
  7.2 2.1 copy-start.4
  7.2 2.2 copy-start.18
  8.8 1.7 copy-start.15
  10.5 327.1 %all-gather.5.cloned.1.call-start = ((), (), s32[]{:S(2)}) async-start(), calls=%async_computation.2 | async-start | bytes 17825792 | tf_op jit(solution)/shard_map/all_gather | solution.py:111
  11.6 1.4 copy-start.2
  13.3 2.8 copy-start.5
  14.0 4.2 %copy-start.6 = (bf16[256,256]{1,0:T(8,128)(2,1)S(1)}, bf16[256,256]{1,0:T(8,128)(2,1)}, u32[]{:S(2)}) copy-start(bf16[256,256]{1,0:T(8,128)(2,1)} %param.27) | copy-start | bytes 393220
  114.0 3.0 copy-start.7
  114.0 3.0 copy-start.8
  119.6 9.3 %copy-start.16 = (bf16[128,128]{1,0:T(8,128)(2,1)S(1)}, bf16[128,128]{1,0:T(8,128)(2,1)}, u32[]{:S(2)}) copy-start(bf16[128,128]{1,0:T(8,128)(2,1)} %param.36) | copy-start | bytes 98308
  121.2 44.1 %all-to-all-start = ((bf16[8,256,256]{2,0,1:T(8,128)(2,1)}), bf16[8,256,256]{2,0,1:T(8,128)(2,1)S(1)}, u32[]{:S(2)}, u32[]{:S(2)}) async-start(bf16[8,256,256]{2,0,1:T(8,128)(2,1)} %copy.100), calls=%async_computation | async-start | bytes 2097152 | tf_op jit(solution)/shard_map/all_to_all | solution.py:138
  128.9 2.8 copy-start.19
  165.5 1.0 copy-start.9
  166.5 3.4 copy-start.10
  171.7 2.4 copy-start.11
  193.3 3.0 copy-start.12
  352.8 0.8 copy-start.3
  353.6 0.8 copy-start.17
  354.3 1.5 copy-start.13
  354.4 1.5 copy-start.14
  355.8 3.9 %copy-start.1 = (bf16[256,256]{1,0:T(8,128)(2,1)S(1)}, bf16[256,256]{1,0:T(8,128)(2,1)}, u32[]{:S(2)}) copy-start(bf16[256,256]{1,0:T(8,128)(2,1)} %param.25) | copy-start | bytes 393220
Sparse Core Ops, SparseCore 0:
  10.6 80.1 all-gather.2
  93.4 244.0 all-gather.4
where the time goes:
time: 369 us; the launch traced here: 367 us
  waiting for transfers between devices  241 us (65%)
  matrix products  74.5 us (20%)
  local copies, waits for them, and re-layouts  24.9 us (7%)
  between operations  14.5 us (4%)
  starting transfers between devices  7.81 us (2%)
    all_gather x1, waiting for transfers between devices, shards(): lax.all_gather(jnp.transpose(right, (2, 0, 1)), 'dap', axis=1, tiled=True)  137 us
    all_gather x1, waiting for transfers between devices, shards(): lax.all_gather(jnp.transpose(project(pair_norm, pair_bias_weight), (2, 0,...  70.6 us
    all_to_all x1, waiting for transfers between devices, shards(): lax.all_to_all(alignment_middle, 'dap', split_axis=1, concat_axis=0, tile...  33.6 us
    dot_general x14, matrix products, project(): result = jnp.dot(flattened, weight, preferred_element_type=jnp.float32)  24 us
    sub x2, matrix products, gated_head_attention(): expo = jnp.exp(scores - row_max)  19 us
    dot_general x2, matrix products, gated_head_attention(): jnp.einsum('bhij,bjhd->bihd', probabilities, value_rows, preferred_elemen...  16.5 us
    dot_general x1, matrix products, shards(): jnp.einsum('cik,cjk->cij', left_sides, lax.all_gather(jnp.transpose(right...  15 us
    all_to_all x1, starting transfers between devices, shards(): lax.all_to_all(alignment_middle, 'dap', split_axis=1, concat_axis=0, tile...  7.73 us
  transfers between devices with their start and end apart: 3, of which 3 were waited for; matrix products, arithmetic and copies ran while one was open for 21% of the time, Pallas kernels for 0%

commit v1 on v0

v1 whole, which is shorter than its diff:
```python
import functools

import jax
import jax.numpy as jnp
from jax import lax
from jax.experimental import pallas as pl
from jax.experimental.pallas import tpu as pltpu
from jax.sharding import PartitionSpec as P

MESH = pl.DeviceIdType.MESH
F32 = jnp.float32
BF16 = jnp.bfloat16
N = 16
HEADS = 8
DH = 32
EPSILON = 1e-05
MASKED = -1000000000.0


def mm(a, b):
    return jnp.dot(a, b, preferred_element_type=F32)


def nt(a, b):
    return lax.dot_general(a, b, (((1,), (1,)), ((), ())), preferred_element_type=F32)


def tn(a, b):
    return lax.dot_general(a, b, (((0,), (0,)), ((), ())), preferred_element_type=F32)


def normalize(x):
    center = x - jnp.mean(x, axis=-1, keepdims=True)
    variance = jnp.mean(center * center, axis=-1, keepdims=True)
    return (center * lax.rsqrt(variance + EPSILON)).astype(BF16)


def sigmoid(x):
    return 1.0 / (1.0 + jnp.exp(-x))


def transposed(w):
    return jnp.transpose(w.astype(F32)).astype(BF16)


def attend(k_rows, qz, vt, gt, bias, heads, width, store):
    scores = mm(k_rows, qz) + bias
    top = jnp.max(scores, axis=0, keepdims=True)
    weights = jnp.exp(scores - top).astype(BF16)
    for n, h in enumerate(heads):
        part = weights if len(heads) == 1 else weights[:, n * width : (n + 1) * width]
        mix = mm(vt[h], part)
        gated = mix[:DH] * (1.0 / mix[DH : DH + 1]) * gt[h * DH : (h + 1) * DH]
        store(h, gated.astype(BF16))


def kernel(
    al, pr, rmask_s, rmask, smask,
    rwq, rwk, rwv, rwg, rwo, pbw, cwq, cwk, cwv, cwg, cwo, tlw, trw, tgw, tow, tiw, tww,
    out_al, out_pr,
    pn, lr_t, b_t, send_lr, recv_lr, send_b, recv_b, bias_t, send_m, recv_m, send_c, recv_c,
    wt, wlr, wb, qz, vt, qzc, vtc, gt, gtc, cn, gcol, cnt, gate, swap, eye,
    s_lr, r_lr, s_b, r_b, s_m, r_m, s_c, r_c,
):
    me = lax.axis_index("dap")

    def peer(o):
        return lax.rem(me + o, N)

    barrier = pltpu.get_barrier_semaphore()
    for o in range(1, N):
        pl.semaphore_signal(barrier, inc=1, device_id={"dap": peer(o)}, device_id_type=MESH)

    def copy(src, dst, ssem, rsem, to):
        return pltpu.make_async_remote_copy(
            src_ref=src, dst_ref=dst, send_sem=ssem, recv_sem=rsem,
            device_id={"dap": to}, device_id_type=MESH,
        )

    def send_to(send, recv, ssem, rsem, d):
        return copy(send.at[d], recv.at[me], ssem.at[d], rsem.at[me], d)

    def arrival(send, recv, ssem, rsem, d):
        return copy(send.at[d], recv.at[d], ssem.at[d], rsem.at[d], d)

    def wait_all(send, recv, ssem, rsem):
        @pl.loop(1, N)
        def _(o):
            arrival(send, recv, ssem, rsem, peer(o)).wait_recv()

    row = lax.broadcasted_iota(jnp.int32, (256, 256), 0)
    col = lax.broadcasted_iota(jnp.int32, (256, 256), 1)
    swap[...] = jnp.where(col == (row % 16) * 16 + row // 16, 1.0, 0.0).astype(BF16)
    eye[...] = jnp.where(col == row, 1.0, 0.0).astype(BF16)

    wlr[:128, :] = transposed(tlw[...])
    wlr[128:, :] = transposed(trw[...])
    wb[...] = jnp.zeros_like(wb)
    wb[:, :HEADS] = pbw[...].astype(F32)
    wbt = jnp.transpose(wb[...])[:16].astype(BF16)
    live = rmask[...].astype(F32)

    @pl.loop(0, 16)
    def _(i):
        normed = normalize(pr[i].astype(F32))
        pn[i] = normed
        own = rmask_s[me * 16 + i].astype(F32)
        lr_t[i] = (nt(wlr[...], normed) * (live * own)).astype(BF16)
        b_t[i] = nt(wbt, normed).astype(BF16)

    send_b[...] = mm(swap[...], b_t[...].reshape(256, 256))[:128].astype(BF16).reshape(8, 16, 256)

    pl.semaphore_wait(barrier, N - 1)

    def send_bias(d):
        return copy(send_b, recv_b.at[me], s_b.at[d], r_b.at[me], d)

    for o in range(1, N):
        send_bias(peer(o)).start()
    recv_b[me] = send_b[...]

    def split_group(g):
        at = pl.multiple_of(g * 16, 16)
        for side in range(2):
            block = lr_t[:, pl.ds(side * 128 + at, 16), :].reshape(256, 256)
            swapped = mm(swap[...], block).astype(BF16).reshape(2, 8, 16, 256)
            send_lr[2 * g, side] = swapped[0]
            send_lr[2 * g + 1, side] = swapped[1]

    @pl.loop(1, 8)
    def _(n):
        g = lax.rem(me // 2 + n, 8)
        split_group(g)
        send_to(send_lr, recv_lr, s_lr, r_lr, 2 * g).start()
        send_to(send_lr, recv_lr, s_lr, r_lr, 2 * g + 1).start()

    split_group(me // 2)
    near = me + 1 - 2 * (me % 2)
    send_to(send_lr, recv_lr, s_lr, r_lr, near).start()
    recv_lr[me] = send_lr[me]

    wt[0] = transposed(rwq[...])
    wt[1] = transposed(rwv[...])
    wt[2] = transposed(rwg[...])
    wt[3] = transposed(cwq[...])
    wt[4] = transposed(cwv[...])
    wt[5] = transposed(cwg[...])
    qz[...] = jnp.zeros_like(qz)
    qzc[...] = jnp.zeros_like(qzc)
    vt[:, DH:, :] = jnp.ones((HEADS, 16, 256), BF16)
    vtc[:, DH:, :] = jnp.ones((HEADS, 16, 128), BF16)

    @pl.loop(0, 16)
    def _(i):
        gate[i] = sigmoid(mm(pn[i], tgw[...]))

    wait_all(recv_b, recv_b, s_b, r_b)
    shown = nt(eye[...], jnp.broadcast_to(live, (256, 256)).astype(BF16))
    hidden_keys = (1.0 - shown) * MASKED

    @pl.loop(0, HEADS)
    def _(h):
        bias_t[h] = nt(eye[...], recv_b[:, h].reshape(256, 256)) + hidden_keys

    scale = DH ** (-0.5)

    @pl.loop(0, 8)
    def _(s):
        normed = normalize(al[s].astype(F32))
        q = (nt(wt[0], normed) * scale).astype(BF16)
        v = nt(wt[1], normed).astype(BF16)
        g = sigmoid(nt(wt[2], normed))
        k = mm(normed, rwk[...]).astype(BF16)
        for h in range(HEADS):
            qz[h, h * DH : (h + 1) * DH, :] = q[h * DH : (h + 1) * DH]
            vt[h, :DH, :] = v[h * DH : (h + 1) * DH]

        def store(h, gated):
            gt[h * DH : (h + 1) * DH, :] = gated

        for h in range(HEADS):
            attend(k, qz[h], vt, g, bias_t[h], (h,), 256, store)
        mid = (al[s].astype(F32) + tn(gt[...], rwo[...])).astype(BF16)
        send_m[:, s] = mid.reshape(16, 16, 256)

    for o in range(1, N):
        send_to(send_m, recv_m, s_m, r_m, peer(o)).start()
    recv_m[me] = send_m[me]

    wait_all(send_lr, recv_lr, s_lr, r_lr)

    @pl.loop(0, 8)
    def _(c):
        left = recv_lr[:, 0, c].reshape(256, 256)
        right = recv_lr[:, 1, c].reshape(256, 256)
        send_c[:, c] = nt(left, right).astype(BF16).reshape(16, 16, 256)

    for o in range(1, N):
        send_to(send_c, recv_c, s_c, r_c, peer(o)).start()
    recv_c[me] = send_c[me]

    wait_all(send_m, recv_m, s_m, r_m)

    @pl.loop(0, 8)
    def _(b):
        rows = recv_m[pl.ds(2 * b, 2)].reshape(256, 256).astype(F32)
        at = pl.multiple_of(b * 16, 16)
        cn[:, pl.ds(at, 16), :] = mm(swap[...], normalize(rows)).astype(BF16).reshape(16, 16, 256)

    seen = nt(eye[:128, :128], jnp.broadcast_to(smask[...].astype(F32), (256, 128)).astype(BF16))
    hidden_rows = (1.0 - seen) * MASKED

    @pl.loop(0, 16)
    def _(i):
        normed = cn[i]
        q = (nt(wt[3], normed) * scale).astype(BF16)
        v = nt(wt[4], normed).astype(BF16)
        g = sigmoid(nt(wt[5], normed))
        k = mm(normed, cwk[...]).astype(BF16)
        for h in range(HEADS):
            side = (h % 2) * 128
            qzc[h // 2, h * DH : (h + 1) * DH, side : side + 128] = q[h * DH : (h + 1) * DH]
            vtc[h, :DH, :] = v[h * DH : (h + 1) * DH]

        def store(h, gated):
            gtc[h * DH : (h + 1) * DH, :] = gated

        for h in range(HEADS // 2):
            attend(k, qzc[h], vtc, g, hidden_rows, (2 * h, 2 * h + 1), 128, store)
        gcol[i] = transposed(gtc[...])

    @pl.loop(0, 8)
    def _(b):
        at = pl.multiple_of(b * 16, 16)
        rows = mm(swap[...], gcol[:, pl.ds(at, 16), :].reshape(256, 256)).astype(BF16)
        mid = recv_m[pl.ds(2 * b, 2)].reshape(256, 256).astype(F32)
        out_al[pl.ds(at, 16)] = (mid + mm(rows, cwo[...])).astype(BF16).reshape(16, 16, 256)

    wait_all(send_c, recv_c, s_c, r_c)

    total = jnp.zeros((16, 256), F32)
    total = lax.fori_loop(0, N, lambda d, t: t + jnp.sum(recv_c[d].astype(F32), axis=0), total)
    mean = total * (1.0 / 128)

    def spread(d, t):
        center = recv_c[d].astype(F32) - mean[None]
        return t + jnp.sum(center * center, axis=0)

    variance = lax.fori_loop(0, N, spread, jnp.zeros((16, 256), F32)) * (1.0 / 128)
    rate = lax.rsqrt(variance + EPSILON)

    @pl.loop(0, 8)
    def _(g):
        block = recv_c[pl.ds(2 * g, 2)].reshape(16, 16, 256).astype(F32)
        normed = ((block - mean[None]) * rate[None]).astype(BF16).reshape(256, 256)
        at = pl.multiple_of(g * 16, 16)
        cnt[:, pl.ds(at, 16), :] = mm(swap[...], normed).astype(BF16).reshape(16, 16, 256)

    @pl.loop(0, 16)
    def _(i):
        update = tn(cnt[i], tow[...])
        mid = (pr[i].astype(F32) + update * gate[i]).astype(BF16)
        middle = mid.astype(F32)
        hidden = jnp.maximum(mm(normalize(middle), tiw[...]), 0.0).astype(BF16)
        out_pr[i] = (middle + mm(hidden, tww[...])).astype(BF16)

    @pl.loop(1, N)
    def _(o):
        d = peer(o)
        send_bias(d).wait_send()
        send_to(send_lr, recv_lr, s_lr, r_lr, d).wait_send()
        send_to(send_m, recv_m, s_m, r_m, d).wait_send()
        send_to(send_c, recv_c, s_c, r_c, d).wait_send()


def shards(
    alignment, pair_state, residue_present_mask, alignment_row_mask,
    row_query_weight, row_key_weight, row_value_weight, row_gate_weight, row_output_weight,
    pair_bias_weight,
    column_query_weight, column_key_weight, column_value_weight, column_gate_weight, column_output_weight,
    triangle_left_weight, triangle_right_weight, triangle_gate_weight, triangle_output_weight,
    transition_input_weight, transition_output_weight,
):
    vmem = pl.BlockSpec(memory_space=pltpu.VMEM)
    smem = pl.BlockSpec(memory_space=pltpu.SMEM)
    dma = pltpu.SemaphoreType.DMA((N,))
    return tuple(
        pl.pallas_call(
            kernel,
            out_shape=(
                jax.ShapeDtypeStruct((128, 16, 256), BF16),
                jax.ShapeDtypeStruct((16, 256, 128), BF16),
            ),
            in_specs=[vmem, vmem, smem] + [vmem] * 19,
            out_specs=(vmem, vmem),
            scratch_shapes=[
                pltpu.VMEM((16, 256, 128), BF16),
                pltpu.VMEM((16, 256, 256), BF16),
                pltpu.VMEM((16, 16, 256), BF16),
                pltpu.VMEM((N, 2, 8, 16, 256), BF16),
                pltpu.VMEM((N, 2, 8, 16, 256), BF16),
                pltpu.VMEM((8, 16, 256), BF16),
                pltpu.VMEM((N, 8, 16, 256), BF16),
                pltpu.VMEM((8, 256, 256), F32),
                pltpu.VMEM((N, 8, 16, 256), BF16),
                pltpu.VMEM((N, 8, 16, 256), BF16),
                pltpu.VMEM((N, 8, 16, 256), BF16),
                pltpu.VMEM((N, 8, 16, 256), BF16),
                pltpu.VMEM((6, 256, 256), BF16),
                pltpu.VMEM((256, 128), BF16),
                pltpu.VMEM((128, 128), F32),
                pltpu.VMEM((8, 256, 256), BF16),
                pltpu.VMEM((8, 48, 256), BF16),
                pltpu.VMEM((4, 256, 256), BF16),
                pltpu.VMEM((8, 48, 128), BF16),
                pltpu.VMEM((256, 256), BF16),
                pltpu.VMEM((256, 128), BF16),
                pltpu.VMEM((16, 128, 256), BF16),
                pltpu.VMEM((16, 128, 256), BF16),
                pltpu.VMEM((16, 128, 256), BF16),
                pltpu.VMEM((16, 256, 128), F32),
                pltpu.VMEM((256, 256), BF16),
                pltpu.VMEM((256, 256), BF16),
            ]
            + [dma] * 8,
            compiler_params=pltpu.CompilerParams(
                collective_id=0, has_side_effects=True, vmem_limit_bytes=56 << 20
            ),
        )(
            alignment, pair_state, residue_present_mask,
            residue_present_mask.reshape(1, 256), alignment_row_mask.reshape(1, 128),
            row_query_weight, row_key_weight, row_value_weight, row_gate_weight, row_output_weight,
            pair_bias_weight,
            column_query_weight, column_key_weight, column_value_weight, column_gate_weight,
            column_output_weight,
            triangle_left_weight, triangle_right_weight, triangle_gate_weight, triangle_output_weight,
            transition_input_weight, transition_output_weight,
        )
    )


def solution(mesh):
    in_specs = (
        P(("dp", "dap"), None, None),
        P(("dp", "dap"), None, None),
        P("dp"),
        P("dp"),
    ) + (P(),) * 17
    out_specs = (P("dp", "dap", None), P(("dp", "dap"), None, None))
    return jax.shard_map(shards, mesh=mesh, in_specs=in_specs, out_specs=out_specs, check_vma=False)
```

time: 369 us -> 152 us (0.41)
  waiting for transfers between devices: 241 us -> 0 us
  Pallas kernels: 0 us -> 145 us
  matrix products: 74.5 us -> 0 us
  local copies, waits for them, and re-layouts: 24.9 us -> 4.72 us
  between operations: 14.5 us -> 0.66 us
  starting transfers between devices: 7.81 us -> 0 us
    all_gather x2 -> x0, waiting for transfers between devices: 208 us -> none  [the longest x1 137 us: shards(): lax.all_gather(jnp.transpose(right, (2, 0, 1)), 'dap', axis=1, tiled=True)]
    pallas_call x0 -> x1, Pallas kernels: none -> 145 us  [shards(): pl.pallas_call(kernel, out_shape=(jax.ShapeDtypeStruct((128, 16, 256), BF...]
    dot_general x17 -> x0, matrix products: 55.5 us -> none  [the longest x14 24 us: project(): result = jnp.dot(flattened, weight, preferred_element_type=jnp.float32)]
    all_to_all x1 -> x0, waiting for transfers between devices: 33.6 us -> none  [shards(): lax.all_to_all(alignment_middle, 'dap', split_axis=1, concat_axis=0, tile...]
    sub x2 -> x0, matrix products: 19 us -> none  [gated_head_attention(): expo = jnp.exp(scores - row_max)]
    convert_element_type x7 -> x0, local copies, waits for them, and re-layouts: 13.7 us -> none  [the longest x1 2.83 us: shards(): bias_expanded = pair_bias.astype(jnp.float32)[None]]
    all_to_all x1 -> x0, starting transfers between devices: 7.73 us -> none  [shards(): lax.all_to_all(alignment_middle, 'dap', split_axis=1, concat_axis=0, tile...]
    reshape x2 -> x0, local copies, waits for them, and re-layouts: 5.97 us -> none  [gated_head_attention(): mixture.reshape(batch_rows, length, head_count * DH) * gate_rows]
  transfers between devices with their start and end apart: 3 -> 0, of which waited for: 3 -> 0; matrix products, arithmetic and copies ran while one was open for 21% -> 0% of each run, Pallas kernels for 0% -> 0%
where the time goes in v1:
time: 152 us; the launch traced here: 151 us
  Pallas kernels  145 us (95%)
  local copies, waits for them, and re-layouts  4.72 us (3%)
    pallas_call x1, Pallas kernels, shards(): pl.pallas_call(kernel, out_shape=(jax.ShapeDtypeStruct((128, 16, 256), BF...  145 us
    unnamed x7, local copies, waits for them, and re-layouts  4.72 us

profile of v1, /device:TPU:6, one launch (start us, length us, event | category | flops | bytes accessed | tf_op | source)
XLA Modules:
  0.0 150.7 jit_solution(170685404405996071)
XLA Ops:
  0.6 0.0 copy-start.1
  0.6 0.7 copy-done.1
  1.3 0.7 copy.23.pbw
  2.0 145.4 %shard_map.212 = (bf16[128,16,256]{2,1,0:T(8,128)(2,1)}, bf16[16,256,128]{2,1,0:T(8,128)(2,1)}) custom-call(bf16[8,256,256]{2,1,0:T(8,128)(2,1)} %al.1, bf16[16,256,128]{2,1,0:T(8,128)(2,1)} %pr.1, s32[256]{0:T(256)} %rmask_s.1, s32[1,256]{1,0:T(1,128)} %bitcast.2, s32[1,128]{1,0:T(1,128)} %bitcast.3, bf16[256,256]{1,0:T(8,128)(2,1)} %rwq.1, ...), custom_call_target="tpu_custom_call" | custom-call | tf_op jit(solution)/shard_map/pallas_call | solution.py:288
  147.4 0.0 copy-start
  147.4 2.4 %copy.26 = bf16[128,16,256]{2,1,0:T(8,128)(2,1)} copy(bf16[128,16,256]{2,1,0:T(8,128)(2,1)} %get-tuple-element.4) | data formatting | bytes 2097152
  149.8 0.0 copy-done
  149.8 1.0 copy.27
Async XLA Ops:
  0.6 0.7 copy-start.1
  147.4 2.4 %copy-start = (bf16[16,256,128]{2,1,0:T(8,128)(2,1)S(1)}, bf16[16,256,128]{2,1,0:T(8,128)(2,1)}, u32[]{:S(2)}) copy-start(bf16[16,256,128]{2,1,0:T(8,128)(2,1)} %get-tuple-element.5) | copy-start | bytes 3145732

commit v2 on v1

v2 whole, which is shorter than its diff:
```python
import functools

import jax
import jax.numpy as jnp
from jax import lax
from jax.experimental import pallas as pl
from jax.experimental.pallas import tpu as pltpu
from jax.sharding import PartitionSpec as P

MESH = pl.DeviceIdType.MESH
F32 = jnp.float32
BF16 = jnp.bfloat16
N = 16
HEADS = 8
DH = 32
EPSILON = 1e-05
MASKED = -1000000000.0


def mm(a, b):
    return jnp.dot(a, b, preferred_element_type=F32)


def nt(a, b):
    return lax.dot_general(a, b, (((1,), (1,)), ((), ())), preferred_element_type=F32)


def tn(a, b):
    return lax.dot_general(a, b, (((0,), (0,)), ((), ())), preferred_element_type=F32)


def normalize(x):
    center = x - jnp.mean(x, axis=-1, keepdims=True)
    variance = jnp.mean(center * center, axis=-1, keepdims=True)
    return (center * lax.rsqrt(variance + EPSILON)).astype(BF16)


def sigmoid(x):
    return 1.0 / (1.0 + jnp.exp(-x))


def transposed(w):
    return jnp.transpose(w.astype(F32)).astype(BF16)


def attend(scores, bias, v):
    scores = scores + bias
    top = jnp.max(scores, axis=0, keepdims=True)
    mix = mm(v, jnp.exp(scores - top).astype(BF16))
    return mix[:DH] * (1.0 / mix[DH : DH + 1])


def kernel(
    pr, rmask_s, rmask, smask, pbw, tlw, trw,
    al_h, rwq_h, rwk_h, rwv_h, rwg_h, rwo_h, cwq_h, cwk_h, cwv_h, cwg_h, cwo_h, tgw_h, tow_h, tiw_h, tww_h,
    out_al, out_pr,
    pn, lr_t, b_t, send_lr, recv_lr, recv_b, bias_t, send_m, recv_m, send_c, recv_c,
    wt, wlr, qs, kz, vt, gs, gt, st, st_c, cn, gcol, cnt, gate, swap, eye,
    al, rwq, rwk, rwv, rwg, rwo, cwq, cwk, cwv, cwg, cwo, tgw, tow, tiw, tww, al_v, pr_v,
    s_lr, r_lr, s_b, r_b, s_x, r_x, s_m, r_m, s_c, r_c, s_in, s_out,
):
    me = lax.axis_index("dap")

    def peer(o):
        return lax.rem(me + o, N)

    barrier = pltpu.get_barrier_semaphore()
    for o in range(1, N):
        pl.semaphore_signal(barrier, inc=1, device_id={"dap": peer(o)}, device_id_type=MESH)

    loads = [
        pltpu.make_async_copy(src, dst, s_in.at[n])
        for n, (src, dst) in enumerate(
            zip(
                (rwq_h, rwv_h, rwg_h, cwq_h, cwv_h, cwg_h, tgw_h, al_h, rwk_h, rwo_h, cwk_h, cwo_h, tow_h, tiw_h, tww_h),
                (rwq, rwv, rwg, cwq, cwv, cwg, tgw, al, rwk, rwo, cwk, cwo, tow, tiw, tww),
            )
        )
    ]
    for load in loads:
        load.start()

    def copy(src, dst, ssem, rsem, to):
        return pltpu.make_async_remote_copy(
            src_ref=src, dst_ref=dst, send_sem=ssem, recv_sem=rsem,
            device_id={"dap": to}, device_id_type=MESH,
        )

    def send_to(send, recv, ssem, rsem, d):
        return copy(send.at[d], recv.at[me], ssem.at[d], rsem.at[me], d)

    def arrival(send, recv, ssem, rsem, d):
        return copy(send.at[d], recv.at[d], ssem.at[d], rsem.at[d], d)

    def wait_all(send, recv, ssem, rsem):
        @pl.loop(1, N)
        def _(o):
            arrival(send, recv, ssem, rsem, peer(o)).wait_recv()

    row = lax.broadcasted_iota(jnp.int32, (256, 256), 0)
    col = lax.broadcasted_iota(jnp.int32, (256, 256), 1)
    swap[...] = jnp.where(col == (row % 16) * 16 + row // 16, 1.0, 0.0).astype(BF16)
    eye[...] = jnp.where(col == row, 1.0, 0.0).astype(BF16)

    wlr[:128, :] = transposed(tlw[...])
    wlr[128:, :] = transposed(trw[...])
    live = rmask[...].astype(F32)

    b_t[...] = jnp.zeros_like(b_t)

    @pl.loop(0, 16, unroll=4)
    def _(i):
        normed = normalize(pr[i].astype(F32))
        pn[i] = normed
        own = rmask_s[me * 16 + i].astype(F32)
        lr_t[i] = (nt(wlr[...], normed) * (live * own)).astype(BF16)
        b_t[i, :HEADS] = nt(pbw[...], normed).astype(BF16)

    recv_b[me] = mm(swap[...], b_t[...].reshape(256, 256))[:128].astype(BF16).reshape(8, 16, 256)

    pl.semaphore_wait(barrier, N - 1)

    high = me // 8
    depth = lax.rem(me, 8)

    def along(dz):
        return high * 8 + lax.rem(depth + dz + 8, 8)

    across = lax.rem(me + 8, N)

    def pass_bias(n, origin, to):
        return copy(recv_b.at[origin], recv_b.at[origin], s_b.at[n], r_b.at[origin], to)

    def pass_across(origin):
        return copy(recv_b.at[origin], recv_b.at[origin], s_x.at[origin], r_b.at[origin], across)

    first_hops = [pass_bias(n, me, along(dz)) for n, dz in enumerate((1, -1, 2, -2))]
    second_hops = [
        pass_bias(4 + n, along(at), along(to)) for n, (at, to) in enumerate(((-2, 1), (2, -1), (-2, 2)))
    ]
    for hop in first_hops:
        hop.start()
    pass_across(me).start()

    def split_group(g):
        at = pl.multiple_of(g * 16, 16)
        for side in range(2):
            block = lr_t[:, pl.ds(side * 128 + at, 16), :].reshape(256, 256)
            swapped = mm(swap[...], block).astype(BF16).reshape(2, 8, 16, 256)
            send_lr[2 * g, side] = swapped[0]
            send_lr[2 * g + 1, side] = swapped[1]

    def send_group(n):
        g = lax.rem(me // 2 + n, 8)
        split_group(g)
        send_to(send_lr, recv_lr, s_lr, r_lr, 2 * g).start()
        send_to(send_lr, recv_lr, s_lr, r_lr, 2 * g + 1).start()

    @pl.loop(1, 3)
    def _(n):
        send_group(n)

    for n, w in enumerate((rwq, rwv, rwg, cwq, cwv, cwg)):
        loads[n].wait()
        wt[n] = transposed(w[...])

    for dz in (2, -2, 1, -1):
        pass_across(along(dz)).wait_recv()
    for hop in second_hops:
        hop.start()
    for dz in (2, -2, 1, -1):
        pass_across(along(dz)).start()

    @pl.loop(3, 8)
    def _(n):
        send_group(n)

    split_group(me // 2)
    near = me + 1 - 2 * (me % 2)
    send_to(send_lr, recv_lr, s_lr, r_lr, near).start()
    recv_lr[me] = send_lr[me]

    vt[:, DH:, :] = jnp.ones((HEADS, 16, 256), BF16)

    loads[6].wait()

    @pl.loop(0, 16, unroll=4)
    def _(i):
        gate[i] = sigmoid(mm(pn[i], tgw[...]))

    for dz in (3, -3, 4):
        pass_across(along(dz)).wait_recv()
        pass_across(along(dz)).start()
    for dz in range(8):
        pass_across((1 - high) * 8 + dz).wait_recv()
    shown = nt(eye[...], jnp.broadcast_to(live, (256, 256)).astype(BF16))
    hidden_keys = (1.0 - shown) * MASKED

    @pl.loop(0, HEADS, unroll=2)
    def _(h):
        bias_t[h] = nt(eye[...], recv_b[:, h].reshape(256, 256)) + hidden_keys

    scale = DH ** (-0.5)
    for load in loads[7:]:
        load.wait()

    lane_head = lax.broadcasted_iota(jnp.int32, (256, 256), 1) // DH

    def project(normed, first, wk):
        qs[...] = (nt(wt[first], normed) * scale).astype(BF16)
        v = nt(wt[first + 1], normed).astype(BF16)
        gs[...] = sigmoid(nt(wt[first + 2], normed))
        for h in range(HEADS):
            vt[h, :DH, :] = v[h * DH : (h + 1) * DH]
        return mm(normed, wk[...])

    @pl.loop(0, 8)
    def _(s):
        k = project(normalize(al[s].astype(F32)), 0, rwk)
        for h in range(HEADS):
            kz[h * 256 : (h + 1) * 256, :] = jnp.where(lane_head == h, k, 0.0).astype(BF16)
        st[...] = mm(kz[...], qs[...])
        for h in range(HEADS):
            own = slice(h * DH, (h + 1) * DH)
            gt[own, :] = (attend(st[h * 256 : (h + 1) * 256, :], bias_t[h], vt[h]) * gs[own, :]).astype(BF16)
        mid = (al[s].astype(F32) + tn(gt[...], rwo[...])).astype(BF16)
        send_m[:, s] = mid.reshape(16, 16, 256)

    for o in range(1, N):
        send_to(send_m, recv_m, s_m, r_m, peer(o)).start()
    recv_m[me] = send_m[me]

    wait_all(send_lr, recv_lr, s_lr, r_lr)

    def send_half(n, d):
        return copy(send_c.at[n, d], recv_c.at[n, me], s_c.at[n, d], r_c.at[n, me], d)

    for n in range(2):

        @pl.loop(0, 8, unroll=2)
        def _(c):
            left = recv_lr[:, 0, c].reshape(256, 256)
            right = recv_lr[n * 8 : n * 8 + 8, 1, c].reshape(128, 256)
            send_c[n, :, c] = nt(left, right).astype(BF16).reshape(16, 16, 128)

        for o in range(1, N):
            send_half(n, peer(o)).start()
        recv_c[n, me] = send_c[n, me]

    wait_all(send_m, recv_m, s_m, r_m)

    @pl.loop(0, 8)
    def _(b):
        rows = recv_m[pl.ds(2 * b, 2)].reshape(256, 256).astype(F32)
        at = pl.multiple_of(b * 16, 16)
        cn[:, pl.ds(at, 16), :] = mm(swap[...], normalize(rows)).astype(BF16).reshape(16, 16, 256)

    seen = nt(eye[:128, :128], jnp.broadcast_to(smask[...].astype(F32), (128, 128)).astype(BF16))
    hidden_rows = (1.0 - seen) * MASKED

    @pl.loop(0, 8)
    def _(p):
        k = project(cn[pl.ds(2 * p, 2)].reshape(256, 256), 3, cwk)
        for h in range(HEADS):
            one = jnp.where(lane_head == h, k, 0.0).astype(BF16)
            kz[h * 128 : (h + 1) * 128, :] = one[:128]
            kz[1024 + h * 128 : 1024 + (h + 1) * 128, :] = one[128:]
        for n in range(2):
            half = slice(n * 128, n * 128 + 128)
            st_c[n] = mm(kz[n * 1024 : (n + 1) * 1024, :], qs[:, half])
        for n in range(2):
            half = slice(n * 128, n * 128 + 128)
            for h in range(HEADS):
                own = slice(h * DH, (h + 1) * DH)
                mixed = attend(st_c[n, h * 128 : (h + 1) * 128, :], hidden_rows, vt[h, :, half])
                gt[own, half] = (mixed * gs[own, half]).astype(BF16)
        for n in range(2):
            gcol[2 * p + n] = transposed(gt[:, n * 128 : n * 128 + 128])

    @pl.loop(0, 8)
    def _(b):
        at = pl.multiple_of(b * 16, 16)
        rows = mm(swap[...], gcol[:, pl.ds(at, 16), :].reshape(256, 256)).astype(BF16)
        mid = recv_m[pl.ds(2 * b, 2)].reshape(256, 256).astype(F32)
        al_v[pl.ds(at, 16)] = (mid + mm(rows, cwo[...])).astype(BF16).reshape(16, 16, 256)

    out_rows = pltpu.make_async_copy(al_v, out_al, s_out.at[0])
    out_rows.start()

    pair_out = [
        pltpu.make_async_copy(
            pr_v.at[:, pl.ds(n * 128, 128), :], out_pr.at[:, pl.ds(n * 128, 128), :], s_out.at[1 + n]
        )
        for n in range(2)
    ]
    for n in range(2):

        @pl.loop(1, N)
        def _(o):
            d = peer(o)
            copy(send_c.at[n, d], recv_c.at[n, d], s_c.at[n, d], r_c.at[n, d], d).wait_recv()

        def add(d, t):
            return t + jnp.sum(recv_c[n, d].astype(F32), axis=0)

        mean = lax.fori_loop(0, N, add, jnp.zeros((16, 128), F32), unroll=8) * (1.0 / 128)

        def spread(d, t):
            center = recv_c[n, d].astype(F32) - mean[None]
            return t + jnp.sum(center * center, axis=0)

        variance = lax.fori_loop(0, N, spread, jnp.zeros((16, 128), F32), unroll=8) * (1.0 / 128)
        rate = lax.rsqrt(variance + EPSILON)

        @pl.loop(0, 8, unroll=8)
        def _(g):
            block = recv_c[n, pl.ds(2 * g, 2)].reshape(16, 16, 128).astype(F32)
            normed = ((block - mean[None]) * rate[None]).astype(BF16).reshape(256, 128)
            at = pl.multiple_of(g * 16, 16)
            cnt[:, pl.ds(at, 16), :] = mm(swap[...], normed).astype(BF16).reshape(16, 16, 128)

        span = slice(n * 128, n * 128 + 128)

        @pl.loop(0, 2)
        def _(b):
            some = pl.ds(8 * b, 8)
            update = jnp.concatenate([tn(cnt[8 * b + m], tow[...]) for m in range(8)], axis=0)
            old = pr[some, span, :].reshape(1024, 128).astype(F32)
            mid = (old + update * gate[some, span, :].reshape(1024, 128)).astype(BF16)
            middle = mid.astype(F32)
            hidden = jnp.maximum(mm(normalize(middle), tiw[...]), 0.0).astype(BF16)
            pr_v[some, span, :] = (middle + mm(hidden, tww[...])).astype(BF16).reshape(8, 128, 128)

        pair_out[n].start()

    for hop in first_hops + second_hops:
        hop.wait_send()
    for dz in range(8):
        pass_across(high * 8 + dz).wait_send()

    @pl.loop(1, N)
    def _(o):
        d = peer(o)
        send_to(send_lr, recv_lr, s_lr, r_lr, d).wait_send()
        send_to(send_m, recv_m, s_m, r_m, d).wait_send()
        send_half(0, d).wait_send()
        send_half(1, d).wait_send()

    out_rows.wait()
    for done in pair_out:
        done.wait()


def shards(
    alignment, pair_state, residue_present_mask, alignment_row_mask,
    row_query_weight, row_key_weight, row_value_weight, row_gate_weight, row_output_weight,
    pair_bias_weight,
    column_query_weight, column_key_weight, column_value_weight, column_gate_weight, column_output_weight,
    triangle_left_weight, triangle_right_weight, triangle_gate_weight, triangle_output_weight,
    transition_input_weight, transition_output_weight,
):
    vmem = pl.BlockSpec(memory_space=pltpu.VMEM)
    smem = pl.BlockSpec(memory_space=pltpu.SMEM)
    hbm = pl.BlockSpec(memory_space=pl.ANY)
    dma = pltpu.SemaphoreType.DMA((N,))
    return tuple(
        pl.pallas_call(
            kernel,
            out_shape=(
                jax.ShapeDtypeStruct((128, 16, 256), BF16),
                jax.ShapeDtypeStruct((16, 256, 128), BF16),
            ),
            in_specs=[vmem, smem] + [vmem] * 5 + [hbm] * 15,
            out_specs=(hbm, hbm),
            scratch_shapes=[
                pltpu.VMEM((16, 256, 128), BF16),
                pltpu.VMEM((16, 256, 256), BF16),
                pltpu.VMEM((16, 16, 256), BF16),
                pltpu.VMEM((N, 2, 8, 16, 256), BF16),
                pltpu.VMEM((N, 2, 8, 16, 256), BF16),
                pltpu.VMEM((N, 8, 16, 256), BF16),
                pltpu.VMEM((8, 256, 256), F32),
                pltpu.VMEM((N, 8, 16, 256), BF16),
                pltpu.VMEM((N, 8, 16, 256), BF16),
                pltpu.VMEM((2, N, 8, 16, 128), BF16),
                pltpu.VMEM((2, N, 8, 16, 128), BF16),
                pltpu.VMEM((6, 256, 256), BF16),
                pltpu.VMEM((256, 128), BF16),
                pltpu.VMEM((256, 256), BF16),
                pltpu.VMEM((2048, 256), BF16),
                pltpu.VMEM((8, 48, 256), BF16),
                pltpu.VMEM((256, 256), F32),
                pltpu.VMEM((256, 256), BF16),
                pltpu.VMEM((2048, 256), F32),
                pltpu.VMEM((2, 1024, 128), F32),
                pltpu.VMEM((16, 128, 256), BF16),
                pltpu.VMEM((16, 128, 256), BF16),
                pltpu.VMEM((16, 128, 128), BF16),
                pltpu.VMEM((16, 256, 128), F32),
                pltpu.VMEM((256, 256), BF16),
                pltpu.VMEM((256, 256), BF16),
            ]
            + [pltpu.VMEM((8, 256, 256), BF16)]
            + [pltpu.VMEM((256, 256), BF16)] * 10
            + [pltpu.VMEM((128, 128), BF16)] * 2
            + [
                pltpu.VMEM((128, 512), BF16),
                pltpu.VMEM((512, 128), BF16),
                pltpu.VMEM((128, 16, 256), BF16),
                pltpu.VMEM((16, 256, 128), BF16),
            ]
            + [dma] * 8
            + [pltpu.SemaphoreType.DMA((2, N))] * 2
            + [dma, pltpu.SemaphoreType.DMA((3,))],
            compiler_params=pltpu.CompilerParams(
                collective_id=0, has_side_effects=True, vmem_limit_bytes=56 << 20
            ),
        )(
            pair_state, residue_present_mask,
            residue_present_mask.reshape(1, 256), alignment_row_mask.reshape(1, 128),
            pair_bias_weight.T, triangle_left_weight, triangle_right_weight,
            alignment,
            row_query_weight, row_key_weight, row_value_weight, row_gate_weight, row_output_weight,
            column_query_weight, column_key_weight, column_value_weight, column_gate_weight,
            column_output_weight,
            triangle_gate_weight, triangle_output_weight,
            transition_input_weight, transition_output_weight,
        )
    )


def solution(mesh):
    in_specs = (
        P(("dp", "dap"), None, None),
        P(("dp", "dap"), None, None),
        P("dp"),
        P("dp"),
    ) + (P(),) * 17
    out_specs = (P("dp", "dap", None), P(("dp", "dap"), None, None))
    return jax.shard_map(shards, mesh=mesh, in_specs=in_specs, out_specs=out_specs, check_vma=False)
```

time: 152 us -> 126 us (0.83)
  Pallas kernels: 145 us -> 122 us
    pallas_call x1, Pallas kernels: 145 us -> 122 us  [shards(): pl.pallas_call(kernel, out_shape=(jax.ShapeDtypeStruct((128, 16, 256), BF...]
    unnamed x7 -> x4, local copies, waits for them, and re-layouts: 4.72 us -> 3.32 us
where the time goes in v2:
time: 126 us
  Pallas kernels  122 us (97%)
  local copies, waits for them, and re-layouts  3.32 us (3%)
    pallas_call x1, Pallas kernels, shards(): pl.pallas_call(kernel, out_shape=(jax.ShapeDtypeStruct((128, 16, 256), BF...  122 us
    unnamed x4, local copies, waits for them, and re-layouts  3.32 us

profile of v2, /device:TPU:6, one launch (start us, length us, event | category | flops | bytes accessed | tf_op | source)
XLA Modules:
  0.0 125.9 jit_solution(15874850427821351648)
XLA Ops:
  0.6 121.9 %shard_map.212 = (bf16[128,16,256]{2,1,0:T(8,128)(2,1)}, bf16[16,256,128]{2,1,0:T(8,128)(2,1)}) custom-call(bf16[16,256,128]{2,1,0:T(8,128)(2,1)} %pr.1, s32[256]{0:T(256)} %rmask_s.1, s32[1,256]{1,0:T(1,128)} %bitcast.3, s32[1,128]{1,0:T(1,128)} %bitcast.5, bf16[8,128]{1,0:T(8,128)(2,1)} %bitcast.4, bf16[128,128]{1,0:T(8,128)(2,1)} %tlw.1, ...), custom_call_target="tpu_custom_call" | custom-call | tf_op jit(solution)/shard_map/pallas_call | solution.py:367
  122.6 0.0 copy-start
  122.6 2.4 %copy.25 = bf16[128,16,256]{2,1,0:T(8,128)(2,1)} copy(bf16[128,16,256]{2,1,0:T(8,128)(2,1)} %get-tuple-element.4) | data formatting | bytes 2097152
  125.0 0.0 copy-done
  125.0 1.0 copy.26
Async XLA Ops:
  122.6 2.4 %copy-start = (bf16[16,256,128]{2,1,0:T(8,128)(2,1)S(1)}, bf16[16,256,128]{2,1,0:T(8,128)(2,1)}, u32[]{:S(2)}) copy-start(bf16[16,256,128]{2,1,0:T(8,128)(2,1)} %get-tuple-element.5) | copy-start | bytes 3145732

commit v3 on v2

--- a/solution.py
+++ b/solution.py
@@ -11,6 +11,7 @@
 F32 = jnp.float32
 BF16 = jnp.bfloat16
 N = 16
+AHEAD = 3
 HEADS = 8
 DH = 32
 EPSILON = 1e-05
@@ -32,6 +33,12 @@
 def normalize(x):
     center = x - jnp.mean(x, axis=-1, keepdims=True)
     variance = jnp.mean(center * center, axis=-1, keepdims=True)
+    return (center * lax.rsqrt(variance + EPSILON)).astype(BF16)
+
+
+def normalize_rows(x, average):
+    center = x.astype(F32) - mm(x, average)
+    variance = mm((center * center).astype(BF16), average)
     return (center * lax.rsqrt(variance + EPSILON)).astype(BF16)
 
 
@@ -55,9 +62,9 @@
     al_h, rwq_h, rwk_h, rwv_h, rwg_h, rwo_h, cwq_h, cwk_h, cwv_h, cwg_h, cwo_h, tgw_h, tow_h, tiw_h, tww_h,
     out_al, out_pr,
     pn, lr_t, b_t, send_lr, recv_lr, recv_b, bias_t, send_m, recv_m, send_c, recv_c,
-    wt, wlr, qs, kz, vt, gs, gt, st, st_c, cn, gcol, cnt, gate, swap, eye,
+    wt, wlr, qs, kz, vt, gs, gt, st, st_c, cn, gcol, cnt, gate, swap, eye, average,
     al, rwq, rwk, rwv, rwg, rwo, cwq, cwk, cwv, cwg, cwo, tgw, tow, tiw, tww, al_v, pr_v,
-    s_lr, r_lr, s_b, r_b, s_x, r_x, s_m, r_m, s_c, r_c, s_in, s_out,
+    s_lr, r_lr, s_b, r_b, s_x, s_m, r_m, s_c, r_c, s_in, s_out,
 ):
     me = lax.axis_index("dap")
 
@@ -107,14 +114,15 @@
     live = rmask[...].astype(F32)
 
     b_t[...] = jnp.zeros_like(b_t)
-
-    @pl.loop(0, 16, unroll=4)
-    def _(i):
-        normed = normalize(pr[i].astype(F32))
-        pn[i] = normed
+    average[...] = jnp.full((128, 128), 1.0 / 128, BF16)
+    normed_pair = normalize_rows(pr[...].reshape(4096, 128), average[...])
+    pn[...] = normed_pair.reshape(16, 256, 128)
+    heads = nt(pbw[...], normed_pair).astype(BF16)
+    for i in range(16):
         own = rmask_s[me * 16 + i].astype(F32)
-        lr_t[i] = (nt(wlr[...], normed) * (live * own)).astype(BF16)
-        b_t[i, :HEADS] = nt(pbw[...], normed).astype(BF16)
+        rows = slice(i * 256, i * 256 + 256)
+        lr_t[i] = (nt(wlr[...], normed_pair[rows]) * (live * own)).astype(BF16)
+        b_t[i, :HEADS] = heads[:, rows]
 
     recv_b[me] = mm(swap[...], b_t[...].reshape(256, 256))[:128].astype(BF16).reshape(8, 16, 256)
 
@@ -156,7 +164,7 @@
         send_to(send_lr, recv_lr, s_lr, r_lr, 2 * g).start()
         send_to(send_lr, recv_lr, s_lr, r_lr, 2 * g + 1).start()
 
-    @pl.loop(1, 3)
+    @pl.loop(1, AHEAD)
     def _(n):
         send_group(n)
 
@@ -171,7 +179,7 @@
     for dz in (2, -2, 1, -1):
         pass_across(along(dz)).start()
 
-    @pl.loop(3, 8)
+    @pl.loop(AHEAD, 8)
     def _(n):
         send_group(n)
 
@@ -184,9 +192,7 @@
 
     loads[6].wait()
 
-    @pl.loop(0, 16, unroll=4)
-    def _(i):
-        gate[i] = sigmoid(mm(pn[i], tgw[...]))
+    gate[...] = sigmoid(mm(pn[...].reshape(4096, 128), tgw[...])).reshape(16, 256, 128)
 
     for dz in (3, -3, 4):
         pass_across(along(dz)).wait_recv()
@@ -214,8 +220,11 @@
             vt[h, :DH, :] = v[h * DH : (h + 1) * DH]
         return mm(normed, wk[...])
 
-    @pl.loop(0, 8)
-    def _(s):
+    def send_rows(n, d):
+        some = pl.ds(4 * n, 4)
+        return copy(send_m.at[d, some], recv_m.at[me, some], s_m.at[n, d], r_m.at[n, me], d)
+
+    def row(s):
         k = project(normalize(al[s].astype(F32)), 0, rwk)
         for h in range(HEADS):
             kz[h * 256 : (h + 1) * 256, :] = jnp.where(lane_head == h, k, 0.0).astype(BF16)
@@ -226,8 +235,11 @@
         mid = (al[s].astype(F32) + tn(gt[...], rwo[...])).astype(BF16)
         send_m[:, s] = mid.reshape(16, 16, 256)
 
-    for o in range(1, N):
-        send_to(send_m, recv_m, s_m, r_m, peer(o)).start()
+    for n in range(2):
+        pl.loop(4 * n, 4 * n + 4)(row)
+        for o in range(1, N):
+            send_rows(n, peer(o)).start()
+
     recv_m[me] = send_m[me]
 
     wait_all(send_lr, recv_lr, s_lr, r_lr)
@@ -247,7 +259,13 @@
             send_half(n, peer(o)).start()
         recv_c[n, me] = send_c[n, me]
 
-    wait_all(send_m, recv_m, s_m, r_m)
+    @pl.loop(1, N)
+    def _(o):
+        d = peer(o)
+        for n in range(2):
+            some = pl.ds(4 * n, 4)
+            copy(send_m.at[d, some], recv_m.at[d, some], s_m.at[n, d], r_m.at[n, d], d).wait_recv()
+
 
     @pl.loop(0, 8)
     def _(b):
@@ -321,15 +339,11 @@
 
         span = slice(n * 128, n * 128 + 128)
 
-        @pl.loop(0, 2)
-        def _(b):
-            some = pl.ds(8 * b, 8)
-            update = jnp.concatenate([tn(cnt[8 * b + m], tow[...]) for m in range(8)], axis=0)
-            old = pr[some, span, :].reshape(1024, 128).astype(F32)
-            mid = (old + update * gate[some, span, :].reshape(1024, 128)).astype(BF16)
-            middle = mid.astype(F32)
-            hidden = jnp.maximum(mm(normalize(middle), tiw[...]), 0.0).astype(BF16)
-            pr_v[some, span, :] = (middle + mm(hidden, tww[...])).astype(BF16).reshape(8, 128, 128)
+        update = jnp.concatenate([tn(cnt[i], tow[...]) for i in range(16)], axis=0)
+        old = pr[:, span, :].reshape(2048, 128).astype(F32)
+        mid = (old + update * gate[:, span, :].reshape(2048, 128)).astype(BF16)
+        hidden = jnp.maximum(mm(normalize_rows(mid, average[...]), tiw[...]), 0.0).astype(BF16)
+        pr_v[:, span, :] = (mid.astype(F32) + mm(hidden, tww[...])).astype(BF16).reshape(16, 128, 128)
 
         pair_out[n].start()
 
@@ -342,7 +356,8 @@
     def _(o):
         d = peer(o)
         send_to(send_lr, recv_lr, s_lr, r_lr, d).wait_send()
-        send_to(send_m, recv_m, s_m, r_m, d).wait_send()
+        send_rows(0, d).wait_send()
+        send_rows(1, d).wait_send()
         send_half(0, d).wait_send()
         send_half(1, d).wait_send()
 
@@ -399,6 +414,7 @@
                 pltpu.VMEM((16, 256, 128), F32),
                 pltpu.VMEM((256, 256), BF16),
                 pltpu.VMEM((256, 256), BF16),
+                pltpu.VMEM((128, 128), BF16),
             ]
             + [pltpu.VMEM((8, 256, 256), BF16)]
             + [pltpu.VMEM((256, 256), BF16)] * 10
@@ -409,8 +425,8 @@
                 pltpu.VMEM((128, 16, 256), BF16),
                 pltpu.VMEM((16, 256, 128), BF16),
             ]
-            + [dma] * 8
-            + [pltpu.SemaphoreType.DMA((2, N))] * 2
+            + [dma] * 5
+            + [pltpu.SemaphoreType.DMA((2, N))] * 4
             + [dma, pltpu.SemaphoreType.DMA((3,))],
             compiler_params=pltpu.CompilerParams(
                 collective_id=0, has_side_effects=True, vmem_limit_bytes=56 << 20

time: 126 us -> 119 us (0.944); the launches traced: 126 us -> 117 us
  Pallas kernels: 122 us -> 113 us
    pallas_call x1, Pallas kernels: 122 us -> 113 us  [shards(): pl.pallas_call(kernel, out_shape=(jax.ShapeDtypeStruct((128, 16, 256), BF...]
where the time goes in v3:
time: 119 us; the launch traced here: 117 us
  Pallas kernels  113 us (95%)
  local copies, waits for them, and re-layouts  3.32 us (3%)
    pallas_call x1, Pallas kernels, shards(): pl.pallas_call(kernel, out_shape=(jax.ShapeDtypeStruct((128, 16, 256), BF...  113 us
    unnamed x4, local copies, waits for them, and re-layouts  3.32 us

profile of v3, /device:TPU:6, one launch (start us, length us, event | category | flops | bytes accessed | tf_op | source)
XLA Modules:
  0.0 117.4 jit_solution(3881184102270353326)
XLA Ops:
  0.6 113.4 %shard_map.212 = (bf16[128,16,256]{2,1,0:T(8,128)(2,1)}, bf16[16,256,128]{2,1,0:T(8,128)(2,1)}) custom-call(bf16[16,256,128]{2,1,0:T(8,128)(2,1)} %pr.1, s32[256]{0:T(256)} %rmask_s.1, s32[1,256]{1,0:T(1,128)} %bitcast.3, s32[1,128]{1,0:T(1,128)} %bitcast.5, bf16[8,128]{1,0:T(8,128)(2,1)} %bitcast.4, bf16[128,128]{1,0:T(8,128)(2,1)} %tlw.1, ...), custom_call_target="tpu_custom_call" | custom-call | tf_op jit(solution)/shard_map/pallas_call | solution.py:382
  114.1 0.0 copy-start
  114.1 2.4 %copy.25 = bf16[128,16,256]{2,1,0:T(8,128)(2,1)} copy(bf16[128,16,256]{2,1,0:T(8,128)(2,1)} %get-tuple-element.4) | data formatting | bytes 2097152
  116.5 0.0 copy-done
  116.5 1.0 copy.26
Async XLA Ops:
  114.1 2.4 %copy-start = (bf16[16,256,128]{2,1,0:T(8,128)(2,1)S(1)}, bf16[16,256,128]{2,1,0:T(8,128)(2,1)}, u32[]{:S(2)}) copy-start(bf16[16,256,128]{2,1,0:T(8,128)(2,1)} %get-tuple-element.5) | copy-start | bytes 3145732

commit v4 on v3

--- a/solution.py
+++ b/solution.py
@@ -57,14 +57,85 @@
     return mix[:DH] * (1.0 / mix[DH : DH + 1])
 
 
+def finish(received, rest, cnt, swap, average, tow, tiw, tww):
+    def add(d, t):
+        return t + jnp.sum(received[d].astype(F32), axis=0)
+
+    mean = lax.fori_loop(0, N, add, jnp.zeros((16, 128), F32), unroll=8) * (1.0 / 128)
+
+    def spread(d, t):
+        center = received[d].astype(F32) - mean[None]
+        return t + jnp.sum(center * center, axis=0)
+
+    variance = lax.fori_loop(0, N, spread, jnp.zeros((16, 128), F32), unroll=8) * (1.0 / 128)
+    rate = lax.rsqrt(variance + EPSILON)
+
+    @pl.loop(0, 8, unroll=8)
+    def _(g):
+        block = received[pl.ds(2 * g, 2)].reshape(16, 16, 128).astype(F32)
+        normed = ((block - mean[None]) * rate[None]).astype(BF16).reshape(256, 128)
+        at = pl.multiple_of(g * 16, 16)
+        cnt[:, pl.ds(at, 16), :] = mm(swap, normed).astype(BF16).reshape(16, 16, 128)
+
+    old, gates = rest()
+    update = jnp.concatenate([tn(cnt[i], tow[...]) for i in range(16)], axis=0)
+    mid = (old.reshape(2048, 128).astype(F32) + update * gates.reshape(2048, 128)).astype(BF16)
+    hidden = jnp.maximum(mm(normalize_rows(mid, average), tiw[...]), 0.0).astype(BF16)
+    return (mid.astype(F32) + mm(hidden, tww[...])).astype(BF16).reshape(16, 128, 128)
+
+
+def constants():
+    row = lax.broadcasted_iota(jnp.int32, (256, 256), 0)
+    col = lax.broadcasted_iota(jnp.int32, (256, 256), 1)
+    swap = jnp.where(col == (row % 16) * 16 + row // 16, 1.0, 0.0).astype(BF16)
+    eye = jnp.where(col == row, 1.0, 0.0).astype(BF16)
+    return swap, eye, jnp.full((128, 128), 1.0 / 128, BF16)
+
+
+def last_half(
+    al_h, first_h, received_h, gate_h, pr_h, tow_h, tiw_h, tww_h, out_al, out_pr,
+    al, first, received, gate, old, tow, tiw, tww, cnt, done, s_in, s_out,
+):
+    half = pl.ds(128, 128)
+    loads = [
+        pltpu.make_async_copy(src, dst, s_in.at[n])
+        for n, (src, dst) in enumerate(
+            (
+                (received_h, received), (tow_h, tow), (pr_h.at[:, half, :], old), (gate_h, gate),
+                (tiw_h, tiw), (tww_h, tww), (al_h, al), (first_h, first),
+            )
+        )
+    ]
+    for load in loads:
+        load.start()
+    swap, _, average = constants()
+    loads[0].wait()
+    stores = [
+        pltpu.make_async_copy(al, out_al, s_out.at[0]),
+        pltpu.make_async_copy(first, out_pr.at[:, pl.ds(0, 128), :], s_out.at[1]),
+        pltpu.make_async_copy(done, out_pr.at[:, half, :], s_out.at[2]),
+    ]
+
+    def rest():
+        for load in loads[1:]:
+            load.wait()
+        stores[0].start()
+        stores[1].start()
+        return old[...], gate[...]
+
+    done[...] = finish(received, rest, cnt, swap, average, tow, tiw, tww)
+    stores[2].start()
+    for store in stores:
+        store.wait()
+
+
 def kernel(
-    pr, rmask_s, rmask, smask, pbw, tlw, trw,
-    al_h, rwq_h, rwk_h, rwv_h, rwg_h, rwo_h, cwq_h, cwk_h, cwv_h, cwg_h, cwo_h, tgw_h, tow_h, tiw_h, tww_h,
-    out_al, out_pr,
+    pr_h, rmask_s_h, rmask_h, smask_h, pbw_h, tlw_h, trw_h, al_h, rwq_h, rwk_h, rwv_h, rwg_h, rwo_h, cwq_h, cwk_h, cwv_h, cwg_h, cwo_h, tgw_h, tow_h, tiw_h, tww_h,
+    out_al, out_pr, out_c, out_gate,
     pn, lr_t, b_t, send_lr, recv_lr, recv_b, bias_t, send_m, recv_m, send_c, recv_c,
     wt, wlr, qs, kz, vt, gs, gt, st, st_c, cn, gcol, cnt, gate, swap, eye, average,
-    al, rwq, rwk, rwv, rwg, rwo, cwq, cwk, cwv, cwg, cwo, tgw, tow, tiw, tww, al_v, pr_v,
-    s_lr, r_lr, s_b, r_b, s_x, s_m, r_m, s_c, r_c, s_in, s_out,
+    al, rwq, rwk, rwv, rwg, rwo, cwq, cwk, cwv, cwg, cwo, tgw, tow, tiw, tww, al_v, pr_v, pr, rmask_s, rmask, smask, pbw, tlw, trw,
+    s_lr, r_lr, s_b, r_b, s_x, s_m, r_m, s_c, r_c, s_in, s_out, s_first,
 ):
     me = lax.axis_index("dap")
 
@@ -75,6 +146,15 @@
     for o in range(1, N):
         pl.semaphore_signal(barrier, inc=1, device_id={"dap": peer(o)}, device_id_type=MESH)
 
+    first_loads = [
+        pltpu.make_async_copy(src, dst, s_first.at[n])
+        for n, (src, dst) in enumerate(
+            zip(
+                (pr_h, tlw_h, trw_h, rmask_s_h, rmask_h, pbw_h, smask_h),
+                (pr, tlw, trw, rmask_s, rmask, pbw, smask),
+            )
+        )
+    ]
     loads = [
         pltpu.make_async_copy(src, dst, s_in.at[n])
         for n, (src, dst) in enumerate(
@@ -84,7 +164,7 @@
             )
         )
     ]
-    for load in loads:
+    for load in first_loads:
         load.start()
 
     def copy(src, dst, ssem, rsem, to):
@@ -104,17 +184,17 @@
         def _(o):
             arrival(send, recv, ssem, rsem, peer(o)).wait_recv()
 
-    row = lax.broadcasted_iota(jnp.int32, (256, 256), 0)
-    col = lax.broadcasted_iota(jnp.int32, (256, 256), 1)
-    swap[...] = jnp.where(col == (row % 16) * 16 + row // 16, 1.0, 0.0).astype(BF16)
-    eye[...] = jnp.where(col == row, 1.0, 0.0).astype(BF16)
-
+    swap[...], eye[...], average[...] = constants()
+
+    for load in first_loads:
+        load.wait()
+    for load in loads:
+        load.start()
     wlr[:128, :] = transposed(tlw[...])
     wlr[128:, :] = transposed(trw[...])
     live = rmask[...].astype(F32)
 
     b_t[...] = jnp.zeros_like(b_t)
-    average[...] = jnp.full((128, 128), 1.0 / 128, BF16)
     normed_pair = normalize_rows(pr[...].reshape(4096, 128), average[...])
     pn[...] = normed_pair.reshape(16, 256, 128)
     heads = nt(pbw[...], normed_pair).astype(BF16)
@@ -193,6 +273,8 @@
     loads[6].wait()
 
     gate[...] = sigmoid(mm(pn[...].reshape(4096, 128), tgw[...])).reshape(16, 256, 128)
+    gate_out = pltpu.make_async_copy(gate.at[:, pl.ds(128, 128), :], out_gate, s_out.at[3])
+    gate_out.start()
 
     for dz in (3, -3, 4):
         pass_across(along(dz)).wait_recv()
@@ -245,7 +327,7 @@
     wait_all(send_lr, recv_lr, s_lr, r_lr)
 
     def send_half(n, d):
-        return copy(send_c.at[n, d], recv_c.at[n, me], s_c.at[n, d], r_c.at[n, me], d)
+        return copy(send_c.at[n, d], (recv_c, out_c)[n].at[me], s_c.at[n, d], r_c.at[n, me], d)
 
     for n in range(2):
 
@@ -257,7 +339,10 @@
 
         for o in range(1, N):
             send_half(n, peer(o)).start()
-        recv_c[n, me] = send_c[n, me]
+
+    recv_c[me] = send_c[0, me]
+    own_c = pltpu.make_async_copy(send_c.at[1, me], out_c.at[me], s_out.at[2])
+    own_c.start()
 
     @pl.loop(1, N)
     def _(o):
@@ -305,47 +390,17 @@
     out_rows = pltpu.make_async_copy(al_v, out_al, s_out.at[0])
     out_rows.start()
 
-    pair_out = [
-        pltpu.make_async_copy(
-            pr_v.at[:, pl.ds(n * 128, 128), :], out_pr.at[:, pl.ds(n * 128, 128), :], s_out.at[1 + n]
-        )
-        for n in range(2)
-    ]
-    for n in range(2):
-
+    def wait_half(n):
         @pl.loop(1, N)
         def _(o):
             d = peer(o)
-            copy(send_c.at[n, d], recv_c.at[n, d], s_c.at[n, d], r_c.at[n, d], d).wait_recv()
-
-        def add(d, t):
-            return t + jnp.sum(recv_c[n, d].astype(F32), axis=0)
-
-        mean = lax.fori_loop(0, N, add, jnp.zeros((16, 128), F32), unroll=8) * (1.0 / 128)
-
-        def spread(d, t):
-            center = recv_c[n, d].astype(F32) - mean[None]
-            return t + jnp.sum(center * center, axis=0)
-
-        variance = lax.fori_loop(0, N, spread, jnp.zeros((16, 128), F32), unroll=8) * (1.0 / 128)
-        rate = lax.rsqrt(variance + EPSILON)
-
-        @pl.loop(0, 8, unroll=8)
-        def _(g):
-            block = recv_c[n, pl.ds(2 * g, 2)].reshape(16, 16, 128).astype(F32)
-            normed = ((block - mean[None]) * rate[None]).astype(BF16).reshape(256, 128)
-            at = pl.multiple_of(g * 16, 16)
-            cnt[:, pl.ds(at, 16), :] = mm(swap[...], normed).astype(BF16).reshape(16, 16, 128)
-
-        span = slice(n * 128, n * 128 + 128)
-
-        update = jnp.concatenate([tn(cnt[i], tow[...]) for i in range(16)], axis=0)
-        old = pr[:, span, :].reshape(2048, 128).astype(F32)
-        mid = (old + update * gate[:, span, :].reshape(2048, 128)).astype(BF16)
-        hidden = jnp.maximum(mm(normalize_rows(mid, average[...]), tiw[...]), 0.0).astype(BF16)
-        pr_v[:, span, :] = (mid.astype(F32) + mm(hidden, tww[...])).astype(BF16).reshape(16, 128, 128)
-
-        pair_out[n].start()
+            copy(send_c.at[n, d], (recv_c, out_c)[n].at[d], s_c.at[n, d], r_c.at[n, d], d).wait_recv()
+
+    wait_half(0)
+    pr_v[...] = finish(recv_c, lambda: (pr[:, :128, :], gate[:, :128, :]), cnt, swap[...], average[...], tow, tiw, tww)
+    pair_out = pltpu.make_async_copy(pr_v, out_pr, s_out.at[1])
+    pair_out.start()
+    wait_half(1)
 
     for hop in first_hops + second_hops:
         hop.wait_send()
@@ -361,8 +416,7 @@
         send_half(0, d).wait_send()
         send_half(1, d).wait_send()
 
-    out_rows.wait()
-    for done in pair_out:
+    for done in (out_rows, pair_out, own_c, gate_out):
         done.wait()
 
 
@@ -374,19 +428,19 @@
     triangle_left_weight, triangle_right_weight, triangle_gate_weight, triangle_output_weight,
     transition_input_weight, transition_output_weight,
 ):
-    vmem = pl.BlockSpec(memory_space=pltpu.VMEM)
-    smem = pl.BlockSpec(memory_space=pltpu.SMEM)
     hbm = pl.BlockSpec(memory_space=pl.ANY)
     dma = pltpu.SemaphoreType.DMA((N,))
-    return tuple(
+    al_done, pr_first, received, gates = (
         pl.pallas_call(
             kernel,
             out_shape=(
                 jax.ShapeDtypeStruct((128, 16, 256), BF16),
-                jax.ShapeDtypeStruct((16, 256, 128), BF16),
+                jax.ShapeDtypeStruct((16, 128, 128), BF16),
+                jax.ShapeDtypeStruct((N, 8, 16, 128), BF16),
+                jax.ShapeDtypeStruct((16, 128, 128), F32),
             ),
-            in_specs=[vmem, smem] + [vmem] * 5 + [hbm] * 15,
-            out_specs=(hbm, hbm),
+            in_specs=[hbm] * 22,
+            out_specs=(hbm,) * 4,
             scratch_shapes=[
                 pltpu.VMEM((16, 256, 128), BF16),
                 pltpu.VMEM((16, 256, 256), BF16),
@@ -398,7 +452,7 @@
                 pltpu.VMEM((N, 8, 16, 256), BF16),
                 pltpu.VMEM((N, 8, 16, 256), BF16),
                 pltpu.VMEM((2, N, 8, 16, 128), BF16),
-                pltpu.VMEM((2, N, 8, 16, 128), BF16),
+                pltpu.VMEM((N, 8, 16, 128), BF16),
                 pltpu.VMEM((6, 256, 256), BF16),
                 pltpu.VMEM((256, 128), BF16),
                 pltpu.VMEM((256, 256), BF16),
@@ -423,11 +477,18 @@
                 pltpu.VMEM((128, 512), BF16),
                 pltpu.VMEM((512, 128), BF16),
                 pltpu.VMEM((128, 16, 256), BF16),
+                pltpu.VMEM((16, 128, 128), BF16),
                 pltpu.VMEM((16, 256, 128), BF16),
+                pltpu.SMEM((256,), jnp.int32),
+                pltpu.VMEM((1, 256), jnp.int32),
+                pltpu.VMEM((1, 128), jnp.int32),
+                pltpu.VMEM((8, 128), BF16),
+                pltpu.VMEM((128, 128), BF16),
+                pltpu.VMEM((128, 128), BF16),
             ]
             + [dma] * 5
             + [pltpu.SemaphoreType.DMA((2, N))] * 4
-            + [dma, pltpu.SemaphoreType.DMA((3,))],
+            + [dma, pltpu.SemaphoreType.DMA((4,)), pltpu.SemaphoreType.DMA((7,))],
             compiler_params=pltpu.CompilerParams(
                 collective_id=0, has_side_effects=True, vmem_limit_bytes=56 << 20
             ),
@@ -443,6 +504,35 @@
             transition_input_weight, transition_output_weight,
         )
     )
+    return tuple(
+        pl.pallas_call(
+            last_half,
+            out_shape=(
+                jax.ShapeDtypeStruct((128, 16, 256), BF16),
+                jax.ShapeDtypeStruct((16, 256, 128), BF16),
+            ),
+            in_specs=[hbm] * 8,
+            out_specs=(hbm, hbm),
+            scratch_shapes=[
+                pltpu.VMEM((128, 16, 256), BF16),
+                pltpu.VMEM((16, 128, 128), BF16),
+                pltpu.VMEM((N, 8, 16, 128), BF16),
+                pltpu.VMEM((16, 128, 128), F32),
+                pltpu.VMEM((16, 128, 128), BF16),
+                pltpu.VMEM((128, 128), BF16),
+                pltpu.VMEM((128, 512), BF16),
+                pltpu.VMEM((512, 128), BF16),
+                pltpu.VMEM((16, 128, 128), BF16),
+                pltpu.VMEM((16, 128, 128), BF16),
+                pltpu.SemaphoreType.DMA((8,)),
+                pltpu.SemaphoreType.DMA((3,)),
+            ],
+            compiler_params=pltpu.CompilerParams(vmem_limit_bytes=56 << 20),
+        )(
+            al_done, pr_first, received, gates, pair_state,
+            triangle_output_weight, transition_input_weight, transition_output_weight,
+        )
+    )
 
 
 def solution(mesh):

time: 119 us -> 117 us (0.983)
  local copies, waits for them, and re-layouts: 3.32 us -> 0 us
  Pallas kernels: 113 us -> 115 us
    pallas_call x0 -> x1, Pallas kernels: none -> 4.78 us  [shards(): pl.pallas_call(last_half, out_shape=(jax.ShapeDtypeStruct((128, 16, 256),...]
    unnamed x4 -> x0, local copies, waits for them, and re-layouts: 3.32 us -> none
    pallas_call x1, Pallas kernels: 113 us -> 111 us  [shards(): pl.pallas_call(kernel, out_shape=(jax.ShapeDtypeStruct((128, 16, 256), BF...]
where the time goes in v4:
time: 117 us; the launch traced here: 116 us
  Pallas kernels  115 us (98%)
    pallas_call x1, Pallas kernels, shards(): pl.pallas_call(kernel, out_shape=(jax.ShapeDtypeStruct((128, 16, 256), BF...  111 us
    pallas_call x1, Pallas kernels, shards(): pl.pallas_call(last_half, out_shape=(jax.ShapeDtypeStruct((128, 16, 256),...  4.78 us

profile of v4, /device:TPU:6, one launch (start us, length us, event | category | flops | bytes accessed | tf_op | source)
XLA Modules:
  0.0 116.0 jit_solution(5882633286184413434)
XLA Ops:
  0.6 110.6 %shard_map.212 = (bf16[128,16,256]{2,1,0:T(8,128)(2,1)}, bf16[16,128,128]{2,1,0:T(8,128)(2,1)}, bf16[16,8,16,128]{3,2,1,0:T(8,128)(2,1)}, f32[16,128,128]{2,1,0:T(8,128)}) custom-call(bf16[16,256,128]{2,1,0:T(8,128)(2,1)} %pr_h.3, s32[256]{0:T(256)} %rmask_s_h.1, s32[1,256]{1,0:T(1,128)} %bitcast.3, s32[1,128]{1,0:T(1,128)} %bitcast.5, ...), custom_call_target="tpu_custom_call" | custom-call | tf_op jit(solution)/shard_map/pallas_call | solution.py:434
  111.2 4.8 %shard_map.213 = (bf16[128,16,256]{2,1,0:T(8,128)(2,1)}, bf16[16,256,128]{2,1,0:T(8,128)(2,1)}) custom-call(bf16[128,16,256]{2,1,0:T(8,128)(2,1)} %get-tuple-element.6.al_h, bf16[16,128,128]{2,1,0:T(8,128)(2,1)} %get-tuple-element.7.first_h, bf16[16,8,16,128]{3,2,1,0:T(8,128)(2,1)} %get-tuple-element.8.received_h, f32[16,128,128]{2,1,0:T(8,128)} %get-tuple-element.9.gate_h, ...), custom_call_target="tpu_custom_call" | custom-call | tf_op jit(solution)/shard_map/pallas_call | solution.py:508

commit v5 on v4

--- a/solution.py
+++ b/solution.py
@@ -57,31 +57,39 @@
     return mix[:DH] * (1.0 / mix[DH : DH + 1])
 
 
-def finish(received, rest, cnt, swap, average, tow, tiw, tww):
+def finish(received, rest, cnt, swap, average, tow, tiw, tww, rows):
+    def both(t):
+        if rows == 16:
+            return t
+        t = t[:8] + t[8:]
+        return jnp.concatenate([t, t], axis=0)
+
     def add(d, t):
         return t + jnp.sum(received[d].astype(F32), axis=0)
 
-    mean = lax.fori_loop(0, N, add, jnp.zeros((16, 128), F32), unroll=8) * (1.0 / 128)
+    mean = both(lax.fori_loop(0, N, add, jnp.zeros((16, 128), F32), unroll=8)) * (1.0 / 128)
 
     def spread(d, t):
         center = received[d].astype(F32) - mean[None]
         return t + jnp.sum(center * center, axis=0)
 
-    variance = lax.fori_loop(0, N, spread, jnp.zeros((16, 128), F32), unroll=8) * (1.0 / 128)
+    variance = both(lax.fori_loop(0, N, spread, jnp.zeros((16, 128), F32), unroll=8)) * (1.0 / 128)
     rate = lax.rsqrt(variance + EPSILON)
-
-    @pl.loop(0, 8, unroll=8)
+    channels = 256 // rows
+    senders = channels // 8
+
+    @pl.loop(0, 128 // channels, unroll=True)
     def _(g):
-        block = received[pl.ds(2 * g, 2)].reshape(16, 16, 128).astype(F32)
+        block = received[pl.ds(senders * g, senders)].reshape(16, 16, 128).astype(F32)
         normed = ((block - mean[None]) * rate[None]).astype(BF16).reshape(256, 128)
-        at = pl.multiple_of(g * 16, 16)
-        cnt[:, pl.ds(at, 16), :] = mm(swap, normed).astype(BF16).reshape(16, 16, 128)
+        at = pl.multiple_of(g * channels, channels)
+        cnt[:rows, pl.ds(at, channels), :] = mm(swap, normed).astype(BF16).reshape(rows, channels, 128)
 
     old, gates = rest()
-    update = jnp.concatenate([tn(cnt[i], tow[...]) for i in range(16)], axis=0)
-    mid = (old.reshape(2048, 128).astype(F32) + update * gates.reshape(2048, 128)).astype(BF16)
+    update = jnp.concatenate([tn(cnt[i], tow[...]) for i in range(rows)], axis=0)
+    mid = (old.reshape(rows * 128, 128).astype(F32) + update * gates.reshape(rows * 128, 128)).astype(BF16)
     hidden = jnp.maximum(mm(normalize_rows(mid, average), tiw[...]), 0.0).astype(BF16)
-    return (mid.astype(F32) + mm(hidden, tww[...])).astype(BF16).reshape(16, 128, 128)
+    return (mid.astype(F32) + mm(hidden, tww[...])).astype(BF16).reshape(rows, 128, 128)
 
 
 def constants():
@@ -89,52 +97,58 @@
     col = lax.broadcasted_iota(jnp.int32, (256, 256), 1)
     swap = jnp.where(col == (row % 16) * 16 + row // 16, 1.0, 0.0).astype(BF16)
     eye = jnp.where(col == row, 1.0, 0.0).astype(BF16)
-    return swap, eye, jnp.full((128, 128), 1.0 / 128, BF16)
-
-
-def last_half(
-    al_h, first_h, received_h, gate_h, pr_h, tow_h, tiw_h, tww_h, out_al, out_pr,
-    al, first, received, gate, old, tow, tiw, tww, cnt, done, s_in, s_out,
+    swap_8 = jnp.where(col == (row % 32) * 8 + row // 32, 1.0, 0.0).astype(BF16)
+    return swap, swap_8, eye, jnp.full((128, 128), 1.0 / 128, BF16)
+
+
+def last_part(
+    al_h, first_h, second_h, received_h, gate_h, pr_h, tow_h, tiw_h, tww_h, out_al, out_pr,
+    al, first, second, received, gate, old, tow, tiw, tww, cnt, done, s_in, s_out,
 ):
+    low, high = pl.ds(0, 8), pl.ds(8, 8)
     half = pl.ds(128, 128)
     loads = [
         pltpu.make_async_copy(src, dst, s_in.at[n])
         for n, (src, dst) in enumerate(
             (
-                (received_h, received), (tow_h, tow), (pr_h.at[:, half, :], old), (gate_h, gate),
-                (tiw_h, tiw), (tww_h, tww), (al_h, al), (first_h, first),
+                (received_h, received), (tow_h, tow), (pr_h.at[high, half, :], old), (gate_h, gate),
+                (tiw_h, tiw), (tww_h, tww), (al_h, al), (first_h, first), (second_h, second),
             )
         )
     ]
     for load in loads:
         load.start()
-    swap, _, average = constants()
+    _, swap_8, _, average = constants()
+    stores = [
+        pltpu.make_async_copy(src, dst, s_out.at[n])
+        for n, (src, dst) in enumerate(
+            (
+                (al, out_al), (first, out_pr.at[:, pl.ds(0, 128), :]),
+                (second, out_pr.at[low, half, :]), (done, out_pr.at[high, half, :]),
+            )
+        )
+    ]
     loads[0].wait()
-    stores = [
-        pltpu.make_async_copy(al, out_al, s_out.at[0]),
-        pltpu.make_async_copy(first, out_pr.at[:, pl.ds(0, 128), :], s_out.at[1]),
-        pltpu.make_async_copy(done, out_pr.at[:, half, :], s_out.at[2]),
-    ]
 
     def rest():
         for load in loads[1:]:
             load.wait()
-        stores[0].start()
-        stores[1].start()
+        for store in stores[:3]:
+            store.start()
         return old[...], gate[...]
 
-    done[...] = finish(received, rest, cnt, swap, average, tow, tiw, tww)
-    stores[2].start()
+    done[...] = finish(received, rest, cnt, swap_8, average, tow, tiw, tww, 8)
+    stores[3].start()
     for store in stores:
         store.wait()
 
 
 def kernel(
     pr_h, rmask_s_h, rmask_h, smask_h, pbw_h, tlw_h, trw_h, al_h, rwq_h, rwk_h, rwv_h, rwg_h, rwo_h, cwq_h, cwk_h, cwv_h, cwg_h, cwo_h, tgw_h, tow_h, tiw_h, tww_h,
-    out_al, out_pr, out_c, out_gate,
-    pn, lr_t, b_t, send_lr, recv_lr, recv_b, bias_t, send_m, recv_m, send_c, recv_c,
-    wt, wlr, qs, kz, vt, gs, gt, st, st_c, cn, gcol, cnt, gate, swap, eye, average,
-    al, rwq, rwk, rwv, rwg, rwo, cwq, cwk, cwv, cwg, cwo, tgw, tow, tiw, tww, al_v, pr_v, pr, rmask_s, rmask, smask, pbw, tlw, trw,
+    out_al, out_pr, out_second, out_c, out_gate,
+    pn, lr_t, b_t, send_lr, recv_lr, recv_b, bias_t, send_m, recv_m, send_c, recv_c, send_q, recv_q,
+    wt, wlr, qs, kz, vt, gs, gt, st, st_c, cn, gcol, cnt, gate, swap, swap_8, eye, average,
+    al, rwq, rwk, rwv, rwg, rwo, cwq, cwk, cwv, cwg, cwo, tgw, tow, tiw, tww, al_v, pr_v, pr_w, pr, rmask_s, rmask, smask, pbw, tlw, trw,
     s_lr, r_lr, s_b, r_b, s_x, s_m, r_m, s_c, r_c, s_in, s_out, s_first,
 ):
     me = lax.axis_index("dap")
@@ -184,14 +198,12 @@
         def _(o):
             arrival(send, recv, ssem, rsem, peer(o)).wait_recv()
 
-    swap[...], eye[...], average[...] = constants()
+    swap[...], swap_8[...], eye[...], average[...] = constants()
 
     for load in first_loads:
         load.wait()
     for load in loads:
         load.start()
-    wlr[:128, :] = transposed(tlw[...])
-    wlr[128:, :] = transposed(trw[...])
     live = rmask[...].astype(F32)
 
     b_t[...] = jnp.zeros_like(b_t)
@@ -199,10 +211,7 @@
     pn[...] = normed_pair.reshape(16, 256, 128)
     heads = nt(pbw[...], normed_pair).astype(BF16)
     for i in range(16):
-        own = rmask_s[me * 16 + i].astype(F32)
-        rows = slice(i * 256, i * 256 + 256)
-        lr_t[i] = (nt(wlr[...], normed_pair[rows]) * (live * own)).astype(BF16)
-        b_t[i, :HEADS] = heads[:, rows]
+        b_t[i, :HEADS] = heads[:, i * 256 : i * 256 + 256]
 
     recv_b[me] = mm(swap[...], b_t[...].reshape(256, 256))[:128].astype(BF16).reshape(8, 16, 256)
 
@@ -230,6 +239,12 @@
         hop.start()
     pass_across(me).start()
 
+    wlr[:128, :] = transposed(tlw[...])
+    wlr[128:, :] = transposed(trw[...])
+    for i in range(16):
+        own = rmask_s[me * 16 + i].astype(F32)
+        lr_t[i] = (nt(wlr[...], pn[i]) * (live * own)).astype(BF16)
+
     def split_group(g):
         at = pl.multiple_of(g * 16, 16)
         for side in range(2):
@@ -273,7 +288,7 @@
     loads[6].wait()
 
     gate[...] = sigmoid(mm(pn[...].reshape(4096, 128), tgw[...])).reshape(16, 256, 128)
-    gate_out = pltpu.make_async_copy(gate.at[:, pl.ds(128, 128), :], out_gate, s_out.at[3])
+    gate_out = pltpu.make_async_copy(gate.at[pl.ds(8, 8), pl.ds(128, 128), :], out_gate, s_out.at[3])
     gate_out.start()
 
     for dz in (3, -3, 4):
@@ -326,22 +341,36 @@
 
     wait_all(send_lr, recv_lr, s_lr, r_lr)
 
-    def send_half(n, d):
-        return copy(send_c.at[n, d], (recv_c, out_c)[n].at[me], s_c.at[n, d], r_c.at[n, me], d)
-
-    for n in range(2):
-
-        @pl.loop(0, 8, unroll=2)
-        def _(c):
-            left = recv_lr[:, 0, c].reshape(256, 256)
-            right = recv_lr[n * 8 : n * 8 + 8, 1, c].reshape(128, 256)
-            send_c[n, :, c] = nt(left, right).astype(BF16).reshape(16, 16, 128)
-
+    sources = (send_c, send_q.at[0], send_q.at[1])
+    targets = (recv_c, recv_q, out_c)
+
+    def send_part(n, d):
+        return copy(sources[n].at[d], targets[n].at[me], s_c.at[n, d], r_c.at[n, me], d)
+
+    def product(c, n):
+        left = recv_lr[:, 0, c].reshape(256, 256)
+        return nt(left, recv_lr[n * 8 : n * 8 + 8, 1, c].reshape(128, 256))
+
+    @pl.loop(0, 8, unroll=2)
+    def _(c):
+        send_c[:, c] = product(c, 0).astype(BF16).reshape(16, 16, 128)
+
+    for o in range(1, N):
+        send_part(0, peer(o)).start()
+
+    @pl.loop(0, 4)
+    def _(c):
+        even = product(2 * c, 1).reshape(16, 2, 8, 128)
+        odd = product(2 * c + 1, 1).reshape(16, 2, 8, 128)
+        for q in range(2):
+            send_q[q, :, c] = jnp.concatenate([even[:, q], odd[:, q]], axis=1).astype(BF16)
+
+    for n in (1, 2):
         for o in range(1, N):
-            send_half(n, peer(o)).start()
-
-    recv_c[me] = send_c[0, me]
-    own_c = pltpu.make_async_copy(send_c.at[1, me], out_c.at[me], s_out.at[2])
+            send_part(n, peer(o)).start()
+    recv_c[me] = send_c[me]
+    recv_q[me] = send_q[0, me]
+    own_c = pltpu.make_async_copy(send_q.at[1, me], out_c.at[me], s_out.at[2])
     own_c.start()
 
     @pl.loop(1, N)
@@ -390,17 +419,25 @@
     out_rows = pltpu.make_async_copy(al_v, out_al, s_out.at[0])
     out_rows.start()
 
-    def wait_half(n):
+    def wait_part(n):
         @pl.loop(1, N)
         def _(o):
             d = peer(o)
-            copy(send_c.at[n, d], (recv_c, out_c)[n].at[d], s_c.at[n, d], r_c.at[n, d], d).wait_recv()
-
-    wait_half(0)
-    pr_v[...] = finish(recv_c, lambda: (pr[:, :128, :], gate[:, :128, :]), cnt, swap[...], average[...], tow, tiw, tww)
+            copy(sources[n].at[d], targets[n].at[d], s_c.at[n, d], r_c.at[n, d], d).wait_recv()
+
+    wait_part(0)
+    pr_v[...] = finish(
+        recv_c, lambda: (pr[:, :128, :], gate[:, :128, :]), cnt, swap[...], average[...], tow, tiw, tww, 16
+    )
     pair_out = pltpu.make_async_copy(pr_v, out_pr, s_out.at[1])
     pair_out.start()
-    wait_half(1)
+    wait_part(1)
+    pr_w[...] = finish(
+        recv_q, lambda: (pr[:8, 128:, :], gate[:8, 128:, :]), cnt, swap_8[...], average[...], tow, tiw, tww, 8
+    )
+    second_out = pltpu.make_async_copy(pr_w, out_second, s_out.at[4])
+    second_out.start()
+    wait_part(2)
 
     for hop in first_hops + second_hops:
         hop.wait_send()
@@ -413,10 +450,10 @@
         send_to(send_lr, recv_lr, s_lr, r_lr, d).wait_send()
         send_rows(0, d).wait_send()
         send_rows(1, d).wait_send()
-        send_half(0, d).wait_send()
-        send_half(1, d).wait_send()
-
-    for done in (out_rows, pair_out, own_c, gate_out):
+        for n in range(3):
+            send_part(n, d).wait_send()
+
+    for done in (out_rows, pair_out, second_out, own_c, gate_out):
         done.wait()
 
 
@@ -430,17 +467,18 @@
 ):
     hbm = pl.BlockSpec(memory_space=pl.ANY)
     dma = pltpu.SemaphoreType.DMA((N,))
-    al_done, pr_first, received, gates = (
+    al_done, first, second, received, gates = (
         pl.pallas_call(
             kernel,
             out_shape=(
                 jax.ShapeDtypeStruct((128, 16, 256), BF16),
                 jax.ShapeDtypeStruct((16, 128, 128), BF16),
-                jax.ShapeDtypeStruct((N, 8, 16, 128), BF16),
-                jax.ShapeDtypeStruct((16, 128, 128), F32),
+                jax.ShapeDtypeStruct((8, 128, 128), BF16),
+                jax.ShapeDtypeStruct((N, 4, 16, 128), BF16),
+                jax.ShapeDtypeStruct((8, 128, 128), F32),
             ),
             in_specs=[hbm] * 22,
-            out_specs=(hbm,) * 4,
+            out_specs=(hbm,) * 5,
             scratch_shapes=[
                 pltpu.VMEM((16, 256, 128), BF16),
                 pltpu.VMEM((16, 256, 256), BF16),
@@ -451,8 +489,10 @@
                 pltpu.VMEM((8, 256, 256), F32),
                 pltpu.VMEM((N, 8, 16, 256), BF16),
                 pltpu.VMEM((N, 8, 16, 256), BF16),
-                pltpu.VMEM((2, N, 8, 16, 128), BF16),
                 pltpu.VMEM((N, 8, 16, 128), BF16),
+                pltpu.VMEM((N, 8, 16, 128), BF16),
+                pltpu.VMEM((2, N, 4, 16, 128), BF16),
+                pltpu.VMEM((N, 4, 16, 128), BF16),
                 pltpu.VMEM((6, 256, 256), BF16),
                 pltpu.VMEM((256, 128), BF16),
                 pltpu.VMEM((256, 256), BF16),
@@ -468,6 +508,7 @@
                 pltpu.VMEM((16, 256, 128), F32),
                 pltpu.VMEM((256, 256), BF16),
                 pltpu.VMEM((256, 256), BF16),
+                pltpu.VMEM((256, 256), BF16),
                 pltpu.VMEM((128, 128), BF16),
             ]
             + [pltpu.VMEM((8, 256, 256), BF16)]
@@ -478,6 +519,7 @@
                 pltpu.VMEM((512, 128), BF16),
                 pltpu.VMEM((128, 16, 256), BF16),
                 pltpu.VMEM((16, 128, 128), BF16),
+                pltpu.VMEM((8, 128, 128), BF16),
                 pltpu.VMEM((16, 256, 128), BF16),
                 pltpu.SMEM((256,), jnp.int32),
                 pltpu.VMEM((1, 256), jnp.int32),
@@ -487,8 +529,9 @@
                 pltpu.VMEM((128, 128), BF16),
             ]
             + [dma] * 5
-            + [pltpu.SemaphoreType.DMA((2, N))] * 4
-            + [dma, pltpu.SemaphoreType.DMA((4,)), pltpu.SemaphoreType.DMA((7,))],
+            + [pltpu.SemaphoreType.DMA((2, N))] * 2
+            + [pltpu.SemaphoreType.DMA((3, N))] * 2
+            + [dma, pltpu.SemaphoreType.DMA((5,)), pltpu.SemaphoreType.DMA((7,))],
             compiler_params=pltpu.CompilerParams(
                 collective_id=0, has_side_effects=True, vmem_limit_bytes=56 << 20
             ),
@@ -506,30 +549,31 @@
     )
     return tuple(
         pl.pallas_call(
-            last_half,
+            last_part,
             out_shape=(
                 jax.ShapeDtypeStruct((128, 16, 256), BF16),
                 jax.ShapeDtypeStruct((16, 256, 128), BF16),
             ),
-            in_specs=[hbm] * 8,
+            in_specs=[hbm] * 9,
             out_specs=(hbm, hbm),
             scratch_shapes=[
                 pltpu.VMEM((128, 16, 256), BF16),
                 pltpu.VMEM((16, 128, 128), BF16),
-                pltpu.VMEM((N, 8, 16, 128), BF16),
-                pltpu.VMEM((16, 128, 128), F32),
-                pltpu.VMEM((16, 128, 128), BF16),
+                pltpu.VMEM((8, 128, 128), BF16),
+                pltpu.VMEM((N, 4, 16, 128), BF16),
+                pltpu.VMEM((8, 128, 128), F32),
+                pltpu.VMEM((8, 128, 128), BF16),
                 pltpu.VMEM((128, 128), BF16),
                 pltpu.VMEM((128, 512), BF16),
                 pltpu.VMEM((512, 128), BF16),
-                pltpu.VMEM((16, 128, 128), BF16),
-                pltpu.VMEM((16, 128, 128), BF16),
-                pltpu.SemaphoreType.DMA((8,)),
-                pltpu.SemaphoreType.DMA((3,)),
+                pltpu.VMEM((8, 128, 128), BF16),
+                pltpu.VMEM((8, 128, 128), BF16),
+                pltpu.SemaphoreType.DMA((9,)),
+                pltpu.SemaphoreType.DMA((4,)),
             ],
             compiler_params=pltpu.CompilerParams(vmem_limit_bytes=56 << 20),
         )(
-            al_done, pr_first, received, gates, pair_state,
+            al_done, first, second, received, gates, pair_state,
             triangle_output_weight, transition_input_weight, transition_output_weight,
         )
     )

time: 117 us -> 116 us (level)
  no operation moved by 1% of the time
where the time goes in v5:
time: 116 us; the launch traced here: 115 us
  Pallas kernels  114 us (98%)
    pallas_call x1, Pallas kernels, shards(): pl.pallas_call(kernel, out_shape=(jax.ShapeDtypeStruct((128, 16, 256), BF...  111 us
    pallas_call x1, Pallas kernels, shards(): pl.pallas_call(last_part, out_shape=(jax.ShapeDtypeStruct((128, 16, 256),...  3.78 us

profile of v5, /device:TPU:6, one launch (start us, length us, event | category | flops | bytes accessed | tf_op | source)
XLA Modules:
  0.0 115.0 jit_solution(4186281511980702131)
XLA Ops:
  0.6 110.5 %shard_map.212 = (bf16[128,16,256]{2,1,0:T(8,128)(2,1)}, bf16[16,128,128]{2,1,0:T(8,128)(2,1)}, bf16[8,128,128]{2,1,0:T(8,128)(2,1)}, bf16[16,4,16,128]{3,2,1,0:T(8,128)(2,1)}, f32[8,128,128]{2,1,0:T(8,128)}) custom-call(bf16[16,256,128]{2,1,0:T(8,128)(2,1)} %pr_h.3, s32[256]{0:T(256)} %rmask_s_h.1, s32[1,256]{1,0:T(1,128)} %bitcast.3, s32[1,128]{1,0:T(1,128)} %bitcast.5, ...), custom_call_target="tpu_custom_call" | custom-call | tf_op jit(solution)/shard_map/pallas_call | solution.py:471
  111.2 3.8 %shard_map.213 = (bf16[128,16,256]{2,1,0:T(8,128)(2,1)}, bf16[16,256,128]{2,1,0:T(8,128)(2,1)}) custom-call(bf16[128,16,256]{2,1,0:T(8,128)(2,1)} %get-tuple-element.7.al_h, bf16[16,128,128]{2,1,0:T(8,128)(2,1)} %get-tuple-element.8.first_h, bf16[8,128,128]{2,1,0:T(8,128)(2,1)} %get-tuple-element.9.second_h, ...), custom_call_target="tpu_custom_call" | custom-call | tf_op jit(solution)/shard_map/pallas_call | solution.py:551
